TPU v7x, 128 devices: a whole 4x4x4 slice. The times are simulated.
128 devices in a mesh: dp: 8 (over z, core), cent: 16 (over x, y).
Axes of the slice: x: 4, y: 4, z: 4, core: 2. Of those that a mesh axis runs over, the one named last changes fastest.
Arguments:
- embeddings: bfloat16 [32768, 1024], P(('dp', 'cent')), may hold values from -6 to 6
- codebook: float32 [16384, 1024], P(('cent', 'dp')), may hold values from -2 to 2
Outputs:
- new_codebook: float32 [16384, 1024], P(('cent', 'dp'))
- counts: float32 [16384], P(('cent', 'dp'))
- log_norm: float32 [32768], P(('dp', 'cent'))
All inputs are finite; a program needn't handle non-finite values.
Results may differ from a plain program's by a relative error of at most 0.0022.
Values may be sent and summed in bfloat16 or wider, within the bound.
A program may use at most 128 MiB of HBM per device.

v0:
```python
import jax
import jax.numpy as jnp
from jax import lax
from jax.sharding import PartitionSpec as P

TEMPER = 0.8
PRIOR = 1.0


def score_block(rows, centers, squares):
    product = lax.dot_general(
        rows, centers, (((1,), (1,)), ((), ())), preferred_element_type=jnp.float32
    )
    return (product - 0.5 * squares[None, :]) / TEMPER


def local(embeddings, codebook):
    own_rows = embeddings.shape[0]
    centers = lax.all_gather(codebook.astype(jnp.bfloat16), "dp", axis=0, tiled=True)
    squares = jnp.sum(jnp.square(centers.astype(jnp.float32)), axis=1)
    gathered = lax.all_gather(embeddings, "cent", axis=0, tiled=True)
    scores = score_block(gathered, centers, squares)
    highest = jnp.max(scores, axis=1)
    summed = jnp.sum(jnp.exp(scores - highest[:, None]), axis=1)
    top_score = lax.pmax(highest, "cent")
    top_total = lax.psum(summed * jnp.exp(highest - top_score), "cent")
    lognorm = top_score + jnp.log(top_total)
    resp = jnp.exp(scores - lognorm[:, None]).astype(jnp.bfloat16)
    tally = jnp.sum(resp.astype(jnp.float32), axis=0)
    sums = lax.dot_general(
        resp, gathered, (((0,), (0,)), ((), ())), preferred_element_type=jnp.float32
    )
    owner_total, owner_tally = (
        lax.psum_scatter(sums, "dp", scatter_dimension=0, tiled=True),
        lax.psum_scatter(tally, "dp", scatter_dimension=0, tiled=True),
    )
    new_codebook = (owner_total + PRIOR * codebook) / (owner_tally + PRIOR)[:, None]
    position = lax.axis_index("cent") * own_rows
    own_norm = lax.dynamic_slice_in_dim(lognorm, position, own_rows, 0)
    return (new_codebook, owner_tally, own_norm)


def solution(mesh):
    return jax.shard_map(
        local,
        mesh=mesh,
        in_specs=(P(("dp", "cent"), None), P(("cent", "dp"), None)),
        out_specs=(P(("cent", "dp"), None), P(("cent", "dp")), P(("dp", "cent"))),
        check_vma=False,
    )
```

profile of v0, /device:TPU:1, one launch (start us, length us, event | category | flops | bytes accessed | tf_op | source)
XLA Modules:
  0.0 339.2 jit_solution(7599833018444706919)
XLA Ops:
  7.2 0.0 all-gather.5.cloned.1.call-start
  7.2 1.8 convert_element_type.12
  9.0 0.0 all-gather.5.cloned.1.call-update
  9.0 0.0 all-gather.3.cloned.1.call-start
  9.1 0.7 all-gather.3.cloned.1.call-update
  9.8 0.0 reduce-scatter.2.cloned.1.call-start
  9.8 29.5 %all-gather.5.cloned.1.call-done = bf16[1024,1024]{1,0:T(8,128)(2,1)} async-done(((bf16[128,1024]{1,0:T(8,128)(2,1)}), bf16[1024,1024]{1,0:T(8,128)(2,1)}) %all-gather.5.cloned.1.call-update) | async-done | bytes 2097168 | tf_op jit(solution)/shard_map/all_gather | solution.py:19
  39.3 2.1 multiply_reduce_fusion
  41.4 70.7 %all-gather.3.cloned.1.call-done = bf16[4096,1024]{1,0:T(8,128)(2,1)} async-done(((bf16[256,1024]{1,0:T(8,128)(2,1)}), bf16[4096,1024]{1,0:T(8,128)(2,1)}) %all-gather.3.cloned.1.call-update) | async-done | bytes 8388624 | tf_op jit(solution)/shard_map/all_gather | solution.py:21
  112.1 16.1 %fusion = (f32[4096]{0:T(1024)S(1)}, f32[4096,1024]{0,1:T(8,128)}) fusion(f32[1024]{0:T(1024)S(1)} %broadcast_multiply_fusion, bf16[4096,1024]{1,0:T(8,128)(2,1)} %all-gather.3.cloned.1.call-done, bf16[1024,1024]{1,0:T(8,128)(2,1)} %all-gather.5.cloned.1.call-done), kind=kOutput, calls=%fused_computation.4 | convolution fusion | flops 8602513408 | bytes 27283456 | tf_op jit(solution)/shard_map/dot_general | solution.py:11
  128.1 58.2 %pmax.7 = f32[4096]{0:T(1024)S(1)} all-reduce(f32[4096]{0:T(1024)S(1)} %get-tuple-element.7), channel_id=1, replica_groups=mesh['dp'=8,'cent'=16] {'cent'}, use_global_device_ids=true, to_apply=%region_2.0 | all-reduce | flops 4096 | bytes 32768 | tf_op jit(solution)/shard_map/pmax | solution.py:25
  186.3 7.7 %exponential_reduce_fusion = f32[4096]{0:T(1024)S(1)} fusion(f32[4096,1024]{0,1:T(8,128)} %get-tuple-element.8, f32[4096]{0:T(1024)S(1)} %get-tuple-element.7, f32[1024]{0:T(1024)S(1)} %broadcast_multiply_fusion), kind=kLoop, calls=%fused_computation.2 | loop fusion | flops 16773120 | bytes 16814080 | tf_op jit(solution)/shard_map/reduce_sum | solution.py:24
  194.1 55.9 %psum.7 = f32[4096]{0:T(1024)S(1)} all-reduce(f32[4096]{0:T(1024)S(1)} %exponential_multiply_fusion), channel_id=1, replica_groups=mesh['dp'=8,'cent'=16] {'cent'}, use_global_device_ids=true, to_apply=%region_4.0 | all-reduce | flops 4096 | bytes 32768 | tf_op jit(solution)/shard_map/psum | solution.py:26
  249.9 8.5 %convert_reduce_fusion = (f32[1024]{0:T(1024)S(1)}, bf16[4096,1024]{0,1:T(8,128)(2,1)S(1)}) fusion(f32[4096]{0:T(1024)S(1)} %log_add_fusion, f32[4096,1024]{0,1:T(8,128)} %get-tuple-element.8, f32[1024]{0:T(1024)S(1)} %broadcast_multiply_fusion), kind=kLoop, calls=%fused_computation | loop fusion | flops 25164800 | bytes 25190400 | tf_op jit(solution)/shard_map/reduce_sum | solution.py:29
  258.4 0.0 copy-start.1
  258.4 0.0 copy-start
  258.4 12.6 %fusion.1 = f32[1024,1024]{1,0:T(8,128)} fusion(bf16[4096,1024]{0,1:T(8,128)(2,1)S(1)} %get-tuple-element.6, bf16[4096,1024]{1,0:T(8,128)(2,1)} %all-gather.3.cloned.1.call-done), kind=kOutput, calls=%fused_computation.11 | convolution fusion | flops 8589934592 | bytes 20971520 | tf_op jit(solution)/shard_map/dot_general | solution.py:30
  271.0 0.0 reduce-scatter.2.cloned.1.call-update
  271.0 0.0 copy-done.1
  271.1 0.6 dynamic-slice
  272.3 0.6 dynamic_slice.3
  272.9 40.6 %all-reduce = f32[1024]{0:T(1024)S(1)} all-reduce(f32[1024]{0:T(1024)S(1)} %get-tuple-element.5), channel_id=3, replica_groups=mesh['dp'=8,'cent'=16] {'dp'}, use_global_device_ids=true, to_apply=%region_7.0.clone | all-reduce | flops 1024 | bytes 8192
  313.5 0.6 broadcast_add_fusion
  314.1 16.6 %reduce-scatter.2.cloned.1.call-done = f32[128,1024]{1,0:T(8,128)} async-done(((f32[1024,1024]{1,0:T(8,128)}), f32[128,1024]{1,0:T(8,128)}) %reduce-scatter.2.cloned.1.call-update) | async-done | bytes 524304 | tf_op jit(solution)/shard_map/reduce_scatter | solution.py:34
  330.7 0.0 copy-done
  330.7 1.9 add_divide_fusion
  (3 shorter events, 0.0 us)
Async XLA Ops:
  7.2 32.2 %all-gather.5.cloned.1.call-start = ((), (), s32[]{:S(2)}) async-start(), calls=%async_computation.2 | async-start | bytes 2359296 | tf_op jit(solution)/shard_map/all_gather | solution.py:19
  9.0 103.1 %all-gather.3.cloned.1.call-start = ((), (), s32[]{:S(2)}) async-start(), calls=%async_computation.1 | async-start | bytes 8912896 | tf_op jit(solution)/shard_map/all_gather | solution.py:21
  9.8 321.0 %reduce-scatter.2.cloned.1.call-start = ((), (), s32[]{:S(2)}) async-start(), calls=%async_computation.3 | async-start | bytes 4718592 | tf_op jit(solution)/shard_map/reduce_scatter | solution.py:34
  258.4 12.6 %copy-start.1 = (u32[128]{0:T(128)S(1)}, u32[128]{0:T(128)}, u32[]{:S(2)}) copy-start(u32[128]{0:T(128)} %constant.23) | copy-start | bytes 1540
  258.4 72.3 %copy-start = (f32[128,1024]{1,0:T(8,128)S(1)}, f32[128,1024]{1,0:T(8,128)}, u32[]{:S(2)}) copy-start(f32[128,1024]{1,0:T(8,128)} %param.3) | copy-start | bytes 1572868
Sparse Core Ops, SparseCore 0:
  10.3 28.9 all-gather.4
  41.5 70.5 all-gather.2
  271.2 59.5 reduce-scatter.1
where the time goes:
time: 342 us; the launch traced here: 339 us
  blocking collectives  155 us (45%)
  waiting for transfers between devices  118 us (35%)
  matrix products  28.7 us (8%)
  other arithmetic  22.6 us (7%)
  between operations  14.5 us (4%)
    all_gather x1, waiting for transfers between devices, local(): gathered = lax.all_gather(embeddings, 'cent', axis=0, tiled=True)  70.7 us
    pmax x1, blocking collectives, local(): top_score = lax.pmax(highest, 'cent')  58.2 us
    psum x1, blocking collectives, local(): top_total = lax.psum(summed * jnp.exp(highest - top_score), 'cent')  55.9 us
    unnamed x1, blocking collectives  40.6 us
    all_gather x1, waiting for transfers between devices, local(): lax.all_gather(codebook.astype(jnp.bfloat16), 'dp', axis=0, tiled=True)  29.5 us
    reduce_scatter x1, waiting for transfers between devices, local(): lax.psum_scatter(sums, 'dp', scatter_dimension=0, tiled=True)  16.6 us
    dot_general x1, matrix products, score_block(): lax.dot_general(rows, centers, (((1,), (1,)), ((), ())), preferred_elemen...  16.1 us
    dot_general x1, matrix products, local(): lax.dot_general(resp, gathered, (((0,), (0,)), ((), ())), preferred_eleme...  12.6 us
  transfers between devices with their start and end apart: 3, of which 3 were waited for; matrix products, arithmetic and copies ran while one was open for 1% of the time, Pallas kernels for 0%

commit v1 on v0

v1 whole, which is shorter than its diff:
```python
import functools
import math

import jax
import jax.numpy as jnp
from jax import lax
from jax.experimental import pallas as pl
from jax.experimental.pallas import tpu as pltpu
from jax.sharding import PartitionSpec as P

TEMPER = 0.8
PRIOR = 1.0
ALPHA = math.log2(math.e) / TEMPER
LN2 = math.log(2.0)
MESH = pl.DeviceIdType.MESH

ROWS, CENTS, WIDTH = 256, 128, 1024
BLOCK = 2 * ROWS
ROW_THIRDS = ((0, 96), (96, 80), (176, 80))
CENT_THIRDS = ((0, 48), (48, 48), (96, 32))
PLACE = {0: 0, 1: 1, 2: 2, 4: 3, 3: 4, 5: 5, 6: 6, 7: 7}
NT = (((1,), (1,)), ((), ()))
NN = (((1,), (0,)), ((), ()))


def waves():
    bit = lambda d: 1 << (d % 3)
    return (
        [(d, d, 0) for d in range(3)],
        [(d, (d - 1) % 3, 0) for d in range(3)],
        [(d, (d - 2) % 3, 0) for d in range(3)],
        [(d, (d - 1) % 3, bit(d - 1)) for d in range(3)],
        [(d, (d - 2) % 3, bit(d - 2)) for d in range(3)],
        [(d, (d - 2) % 3, bit(d - 1)) for d in range(3)],
        [(d, (d - 2) % 3, bit(d - 1) | bit(d - 2)) for d in range(3)],
    )


def combine(terms):
    top = functools.reduce(jnp.maximum, terms)
    total = functools.reduce(jnp.add, [jnp.exp2(t - top) for t in terms])
    return top + jnp.log2(total)


def kernel(
    emb, book, new_out, count_out, norm_out,
    rows, cents, scores, half_sq, peak, sums, tally, lse_all,
    lse_mine, lse_in, part_mine, part_in, fin_in, count_mine, count_in,
    outbox, inbox1, inbox2, inbox3,
    own_sem, row_send, row_recv, sib_send, sib_recv, cent_send, cent_recv,
    stat_send, stat_recv, part_send, part_recv, fin_send, fin_recv,
    count_send, count_recv, sum_send, sum_recv,
):
    dp, cent = lax.axis_index("dp"), lax.axis_index("cent")
    place = (cent // 4, cent % 4, dp // 2)
    core = dp % 2

    def device(p, c):
        return (p[2] * 2 + c, p[0] * 4 + p[1])

    def row_peer(mask, other=0):
        p = [v + 1 - 2 * (v % 2) if mask >> d & 1 else v for d, v in enumerate(place)]
        return device(p, 1 - core if other else core)

    def cent_peer(mask):
        return device([3 - v if mask >> d & 1 else v for d, v in enumerate(place)], core)

    def slot_peer(a):
        return row_peer(a >> 1, a & 1)

    def remote(src, dst, send, recv, to):
        return pltpu.make_async_remote_copy(
            src_ref=src, dst_ref=dst, send_sem=send, recv_sem=recv,
            device_id=to, device_id_type=MESH,
        )

    barrier = pltpu.get_barrier_semaphore()
    peers = [slot_peer(a) for a in range(1, 16)] + [cent_peer(n) for n in range(1, 8)]
    for peer in peers:
        pl.semaphore_signal(barrier, inc=1, device_id=peer, device_id_type=MESH)
    own = pltpu.make_async_copy(emb, rows.at[pl.ds(0, ROWS)], own_sem)
    own.start()
    cents[0:CENTS, :] = book[...].astype(jnp.bfloat16)
    pl.semaphore_wait(barrier, len(peers))

    def row_copy(d, j, m):
        off, size = ROW_THIRDS[j]
        n = m | 1 << d
        dst = rows.at[pl.ds(n * BLOCK + off, size)]
        src = emb.at[pl.ds(off, size)] if m == 0 else rows.at[pl.ds(m * BLOCK + off, size)]
        return remote(src, dst, row_send.at[n, j], row_recv.at[n, j], row_peer(1 << d))

    def cent_copy(d, j, m):
        off, size = CENT_THIRDS[j]
        n = m | 1 << d
        src = cents.at[pl.ds(PLACE[m] * CENTS + off, size)]
        dst = cents.at[pl.ds(PLACE[n] * CENTS + off, size)]
        return remote(src, dst, cent_send.at[n, j], cent_recv.at[n, j], cent_peer(1 << d))

    def sib_copy(n, j):
        off, size = ROW_THIRDS[j]
        src = emb.at[pl.ds(off, size)] if n == 0 else rows.at[pl.ds(n * BLOCK + off, size)]
        dst = rows.at[pl.ds(n * BLOCK + ROWS + off, size)]
        return remote(src, dst, sib_send.at[n, j], sib_recv.at[n, j], row_peer(0, 1))

    wave = waves()

    def row_start(w):
        for msg in wave[w]:
            row_copy(*msg).start()

    def cent_start(w):
        for msg in wave[w]:
            cent_copy(*msg).start()

    def row_arrive(w):
        for d, j, m in wave[w]:
            row_copy(d, j, m).wait_recv()
            sib_copy(m | 1 << d, j).start()

    def cent_arrive(w):
        for msg in wave[w]:
            cent_copy(*msg).wait_recv()

    def sib_arrive(n):
        for j in range(3):
            sib_copy(n, j).wait_recv()

    def squares(half):
        @pl.loop(0, 4)
        def _(i):
            at = pl.ds(pl.multiple_of(half * 512 + i * CENTS, CENTS), CENTS)
            c = cents[at, :].astype(jnp.float32)
            total = jnp.sum(c * c, axis=1, keepdims=True) * (0.5 * ALPHA)
            half_sq[at, :] = jnp.broadcast_to(total, (CENTS, 128))

    def score(n, half):
        if half == 0:
            peak[n] = jnp.full((8, BLOCK), -jnp.inf, jnp.float32)

        @pl.loop(0, 2)
        def _(i):
            at = pl.ds(pl.multiple_of(half * 512 + i * 256, 256), 256)
            product = lax.dot_general(
                cents[at, :], rows[n * BLOCK : (n + 1) * BLOCK, :], NT,
                preferred_element_type=jnp.float32,
            )
            h = half_sq[at, :]
            t = product * ALPHA - jnp.concatenate([h] * (BLOCK // 128), axis=1)
            scores[at, n * BLOCK : (n + 1) * BLOCK] = t
            peak[n] = jnp.maximum(peak[n], jnp.max(t.reshape(32, 8, BLOCK), axis=0))

    def soften(n):
        top = jnp.max(peak[n], axis=0, keepdims=True)

        def body(i, total):
            at = pl.ds(pl.multiple_of(i * 256, 256), 256)
            e = jnp.exp2(scores[at, n * BLOCK : (n + 1) * BLOCK] - top)
            return total + jnp.sum(e.reshape(32, 8, BLOCK), axis=0)

        total = lax.fori_loop(0, 4, body, jnp.zeros((8, BLOCK), jnp.float32))
        lse = top + jnp.log2(jnp.sum(total, axis=0, keepdims=True))
        lse_mine[2 * n] = lse[:, :ROWS]
        lse_mine[2 * n + 1] = lse[:, ROWS:]

    def stat_copy(a):
        return remote(lse_mine.at[a], lse_in.at[a], stat_send.at[a], stat_recv, slot_peer(a))

    def part_copy(a):
        return remote(part_mine, part_in.at[a], part_send.at[a], part_recv, slot_peer(a))

    def fin_copy(a):
        return remote(
            lse_mine.at[pl.ds(12, 4)], fin_in.at[a], fin_send.at[a], fin_recv, slot_peer(a)
        )

    def count_copy(n):
        return remote(count_mine.at[n], count_in.at[n], count_send.at[n], count_recv, cent_peer(n))

    def wait_all(ref, sem):
        remote(ref, ref, own_sem, sem, row_peer(0, 1)).wait_recv()

    cent_start(0)
    row_start(0)
    cent_start(1)
    row_start(1)
    cent_start(2)
    row_start(2)
    for j in range(3):
        sib_copy(0, j).start()
    cent_arrive(0)
    cent_start(3)
    cent_start(4)
    row_arrive(0)
    row_start(3)
    row_start(4)
    cent_arrive(1)
    cent_start(5)
    cent_arrive(2)
    own.wait()
    sib_arrive(0)
    squares(0)
    score(0, 0)
    row_arrive(1)
    row_start(5)
    cent_arrive(3)
    cent_start(6)
    row_arrive(2)
    for n in (1, 2, 4):
        sib_arrive(n)
        score(n, 0)
    cent_arrive(4)
    cent_arrive(5)
    cent_arrive(6)
    squares(1)

    def finish(n):
        score(n, 1)
        soften(n)
        if n < 6:
            for a in (2 * n, 2 * n + 1):
                if a:
                    stat_copy(a).start()

    finish(0)
    row_arrive(3)
    row_start(6)
    finish(1)
    finish(2)
    row_arrive(4)
    finish(4)
    row_arrive(5)
    for n in (3, 5):
        sib_arrive(n)
        score(n, 0)
        finish(n)
    sib_arrive(6)
    score(6, 0)
    finish(6)
    row_arrive(6)
    sib_arrive(7)
    score(7, 0)
    score(7, 1)
    wait_all(lse_in.at[pl.ds(1, 11)], stat_recv)
    part = combine([lse_mine[0]] + [lse_in[a] for a in range(1, 12)])
    part_mine[...] = part
    for a in range(1, 16):
        part_copy(a).start()
    soften(7)
    for a in range(1, 16):
        fin_copy(a).start()
    wait_all(part_in.at[pl.ds(1, 15)], part_recv)
    wait_all(fin_in.at[pl.ds(1, 15)], fin_recv)
    for s in range(16):
        terms = [part_mine[...] if s == 0 else part_in[s]]
        for q in range(12, 16):
            terms.append(lse_mine[q] if s == q else fin_in[s ^ q, q - 12])
        lse = combine(terms)
        lse_all[:, s * ROWS : (s + 1) * ROWS] = lse
        if s == 0:
            norm_out[...] = lse * LN2

    def weigh(n):
        at = PLACE[n] * CENTS
        sums[n] = jnp.zeros((CENTS, WIDTH), jnp.float32)
        tally[...] = jnp.zeros((CENTS, 128), jnp.float32)

        @pl.loop(0, 8)
        def _(r):
            cols = pl.ds(pl.multiple_of(r * BLOCK, BLOCK), BLOCK)
            resp = jnp.exp2(scores[at : at + CENTS, cols] - lse_all[:, cols]).astype(jnp.bfloat16)
            wide = resp.astype(jnp.float32)
            tally[...] += functools.reduce(
                jnp.add, [wide[:, q * 128 : (q + 1) * 128] for q in range(BLOCK // 128)]
            )
            sums[n] += lax.dot_general(resp, rows[cols, :], NN, preferred_element_type=jnp.float32)

        count_mine[n] = jnp.sum(tally[...].T, axis=0, keepdims=True)
        if n:
            count_copy(n).start()

    def step_of(n, j):
        return next(s for s in range(3) if n >> (j + s) % 3 & 1)

    def sum_copy(n, j):
        off, size = CENT_THIRDS[j]
        s = step_of(n, j)
        d = (j + s) % 3
        to = n ^ 1 << d
        box = (inbox1, inbox2, inbox3)[s]
        dst = box.at[0 if s == 2 else to, pl.ds(off, size)]
        return remote(
            outbox.at[n, pl.ds(off, size)], dst, sum_send.at[n, j], sum_recv.at[n, j],
            cent_peer(1 << d),
        )

    def gathered(n, j):
        off, size = CENT_THIRDS[j]
        value = sums[n, off : off + size, :]
        for s in range(step_of(n, j) if n else 3):
            came = n | 1 << (j + s) % 3
            sum_copy(came, j).wait_recv()
            box = (inbox1, inbox2, inbox3)[s]
            value = value + box[0 if s == 2 else n, off : off + size, :].astype(jnp.float32)
        return value

    def send_sums(n, step):
        for j in range(3):
            if step_of(n, j) == step:
                off, size = CENT_THIRDS[j]
                outbox[n, off : off + size, :] = gathered(n, j).astype(jnp.bfloat16)
                sum_copy(n, j).start()

    for n in (7, 3, 6, 5):
        weigh(n)
        send_sums(n, 0)
    for n in (3, 6, 5):
        send_sums(n, 1)
    for n in (1, 2, 4):
        weigh(n)
        send_sums(n, 0)
    for n in (1, 2, 4):
        send_sums(n, 1)
    weigh(0)
    for n in (1, 2, 4):
        send_sums(n, 2)

    for w in range(7):
        for msg in wave[w]:
            row_copy(*msg).wait_send()
            cent_copy(*msg).wait_send()
    for n in range(8):
        for j in range(3):
            sib_copy(n, j).wait_send()
    for a in range(1, 16):
        if a < 12:
            stat_copy(a).wait_send()
        part_copy(a).wait_send()
        fin_copy(a).wait_send()
    wait_all(count_in.at[pl.ds(1, 7)], count_recv)
    count = functools.reduce(jnp.add, [count_mine[0]] + [count_in[n] for n in range(1, 8)])
    count_out[...] = count
    below = jnp.broadcast_to(count, (CENTS, 128)).T + PRIOR
    for j in range(3):
        off, size = CENT_THIRDS[j]
        top = gathered(0, j) + PRIOR * book[off : off + size, :]
        for q in range(WIDTH // 128):
            cols = slice(q * 128, (q + 1) * 128)
            new_out[off : off + size, cols] = top[:, cols] / below[off : off + size, :]
    for n in range(1, 8):
        count_copy(n).wait_send()
        for j in range(3):
            sum_copy(n, j).wait_send()


def local(embeddings, codebook):
    f32, bf16 = jnp.float32, jnp.bfloat16
    vmem, dma = pltpu.VMEM, pltpu.SemaphoreType.DMA
    new, count, norm = pl.pallas_call(
        kernel,
        out_shape=(
            jax.ShapeDtypeStruct((CENTS, WIDTH), f32),
            jax.ShapeDtypeStruct((1, CENTS), f32),
            jax.ShapeDtypeStruct((1, ROWS), f32),
        ),
        in_specs=[pl.BlockSpec(memory_space=pl.ANY), pl.BlockSpec(memory_space=pltpu.VMEM)],
        out_specs=[pl.BlockSpec(memory_space=pltpu.VMEM)] * 3,
        scratch_shapes=[
            vmem((8 * BLOCK, WIDTH), bf16),
            vmem((8 * CENTS, WIDTH), bf16),
            vmem((8 * CENTS, 8 * BLOCK), f32),
            vmem((8 * CENTS, 128), f32),
            vmem((8, 8, BLOCK), f32),
            vmem((8, CENTS, WIDTH), f32),
            vmem((CENTS, 128), f32),
            vmem((1, 8 * BLOCK), f32),
            vmem((16, 1, ROWS), f32),
            vmem((16, 1, ROWS), f32),
            vmem((1, ROWS), f32),
            vmem((16, 1, ROWS), f32),
            vmem((16, 4, 1, ROWS), f32),
            vmem((8, 1, CENTS), f32),
            vmem((8, 1, CENTS), f32),
            vmem((8, CENTS, WIDTH), bf16),
            vmem((8, CENTS, WIDTH), bf16),
            vmem((8, CENTS, WIDTH), bf16),
            vmem((1, CENTS, WIDTH), bf16),
            dma(()),
            dma((8, 3)), dma((8, 3)),
            dma((8, 3)), dma((8, 3)),
            dma((8, 3)), dma((8, 3)),
            dma((16,)), dma(()),
            dma((16,)), dma(()),
            dma((16,)), dma(()),
            dma((8,)), dma(()),
            dma((8, 3)), dma((8, 3)),
        ],
        compiler_params=pltpu.CompilerParams(
            collective_id=0, has_side_effects=True, vmem_limit_bytes=58 * 2**20
        ),
        cost_estimate=pl.CostEstimate(
            flops=4 * 4096 * 1024 * 1024, bytes_accessed=2**21, transcendentals=2**23
        ),
    )(embeddings, codebook)
    return new, count.reshape(CENTS), norm.reshape(ROWS)


def solution(mesh):
    return jax.shard_map(
        local,
        mesh=mesh,
        in_specs=(P(("dp", "cent"), None), P(("cent", "dp"), None)),
        out_specs=(P(("cent", "dp"), None), P(("cent", "dp")), P(("dp", "cent"))),
        check_vma=False,
    )
```

time: 342 us -> 83.3 us (0.24)
  blocking collectives: 155 us -> 0 us
  waiting for transfers between devices: 118 us -> 0 us
  Pallas kernels: 0 us -> 79.4 us
  matrix products: 28.7 us -> 0 us
  other arithmetic: 22.6 us -> 0 us
  between operations: 14.5 us -> 0.65 us
    all_gather x2 -> x0, waiting for transfers between devices: 100 us -> none  [the longest x1 70.7 us: local(): gathered = lax.all_gather(embeddings, 'cent', axis=0, tiled=True)]
    pallas_call x0 -> x1, Pallas kernels: none -> 79.4 us  [local(): pl.pallas_call(kernel, out_shape=(jax.ShapeDtypeStruct((CENTS, WIDTH), f3...]
    pmax x1 -> x0, blocking collectives: 58.2 us -> none  [local(): top_score = lax.pmax(highest, 'cent')]
    psum x1 -> x0, blocking collectives: 55.9 us -> none  [local(): top_total = lax.psum(summed * jnp.exp(highest - top_score), 'cent')]
    unnamed x1 -> x0, blocking collectives: 40.6 us -> none
    dot_general x2 -> x0, matrix products: 28.7 us -> none  [the longest x1 16.1 us: score_block(): lax.dot_general(rows, centers, (((1,), (1,)), ((), ())), preferred_elemen...]
    reduce_sum x3 -> x0, other arithmetic: 18.3 us -> none  [the longest x1 8.46 us: local(): tally = jnp.sum(resp.astype(jnp.float32), axis=0)]
    reduce_scatter x1 -> x0, waiting for transfers between devices: 16.6 us -> none  [local(): lax.psum_scatter(sums, 'dp', scatter_dimension=0, tiled=True)]
  transfers between devices with their start and end apart: 3 -> 0, of which waited for: 3 -> 0; matrix products, arithmetic and copies ran while one was open for 1% -> 0% of each run, Pallas kernels for 0% -> 0%
where the time goes in v1:
time: 83.3 us; the launch traced here: 83.1 us
  Pallas kernels  79.4 us (95%)
  local copies, waits for them, and re-layouts  3.08 us (4%)
    pallas_call x1, Pallas kernels, local(): pl.pallas_call(kernel, out_shape=(jax.ShapeDtypeStruct((CENTS, WIDTH), f3...  79.4 us
    unnamed x7, local copies, waits for them, and re-layouts  3.08 us

profile of v1, /device:TPU:1, one launch (start us, length us, event | category | flops | bytes accessed | tf_op | source)
XLA Modules:
  0.0 83.1 jit_solution(9870467157181294590)
XLA Ops:
  0.6 79.4 %shard_map.49 = (f32[128,1024]{1,0:T(8,128)}, f32[1,128]{1,0:T(1,128)}, f32[1,256]{1,0:T(1,128)}) custom-call(bf16[256,1024]{1,0:T(8,128)(2,1)} %emb.1, f32[128,1024]{1,0:T(8,128)} %book.1), custom_call_target="tpu_custom_call" | custom-call | flops 17179869184 | bytes 2097152 | tf_op jit(solution)/shard_map/pallas_call | solution.py:359
  80.0 0.0 copy-start.1
  80.0 1.9 %copy.8 = f32[128,1024]{1,0:T(8,128)} copy(f32[128,1024]{1,0:T(8,128)} %get-tuple-element.12) | data formatting | bytes 1048576
  81.9 0.0 copy-done.1
  81.9 0.0 copy-start
  81.9 0.5 copy.9
  82.4 0.1 copy-done
  82.6 0.6 copy.10
Async XLA Ops:
  80.0 1.9 %copy-start.1 = (f32[1,128]{1,0:T(1,128)S(1)}, f32[1,128]{1,0:T(1,128)}, u32[]{:S(2)}) copy-start(f32[1,128]{1,0:T(1,128)} %get-tuple-element.7) | copy-start | bytes 1540
  81.9 0.6 copy-start

commit v2 on v1

--- a/solution.py
+++ b/solution.py
@@ -18,7 +18,8 @@
 BLOCK = 2 * ROWS
 ROW_THIRDS = ((0, 96), (96, 80), (176, 80))
 CENT_THIRDS = ((0, 48), (48, 48), (96, 32))
-PLACE = {0: 0, 1: 1, 2: 2, 4: 3, 3: 4, 5: 5, 6: 6, 7: 7}
+ORDER = (0, 1, 2, 4, 3, 5, 6, 7)
+PLACE = {mask: i for i, mask in enumerate(ORDER)}
 NT = (((1,), (1,)), ((), ()))
 NN = (((1,), (0,)), ((), ()))
 
@@ -66,7 +67,7 @@
         return device([3 - v if mask >> d & 1 else v for d, v in enumerate(place)], core)
 
     def slot_peer(a):
-        return row_peer(a >> 1, a & 1)
+        return row_peer(ORDER[a // 2], a % 2)
 
     def remote(src, dst, send, recv, to):
         return pltpu.make_async_remote_copy(
@@ -75,7 +76,7 @@
         )
 
     barrier = pltpu.get_barrier_semaphore()
-    peers = [slot_peer(a) for a in range(1, 16)] + [cent_peer(n) for n in range(1, 8)]
+    peers = [row_peer(0, 1)] + [row_peer(b) for b in (1, 2, 4)] + [cent_peer(b) for b in (1, 2, 4)]
     for peer in peers:
         pl.semaphore_signal(barrier, inc=1, device_id=peer, device_id_type=MESH)
     own = pltpu.make_async_copy(emb, rows.at[pl.ds(0, ROWS)], own_sem)
@@ -83,24 +84,28 @@
     cents[0:CENTS, :] = book[...].astype(jnp.bfloat16)
     pl.semaphore_wait(barrier, len(peers))
 
+    def row_at(n, k, j):
+        off, size = ROW_THIRDS[j]
+        return pl.ds(PLACE[n] * BLOCK + k * ROWS + off, size)
+
+    def cent_at(n, j):
+        off, size = CENT_THIRDS[j]
+        return pl.ds(PLACE[n] * CENTS + off, size)
+
     def row_copy(d, j, m):
-        off, size = ROW_THIRDS[j]
         n = m | 1 << d
-        dst = rows.at[pl.ds(n * BLOCK + off, size)]
-        src = emb.at[pl.ds(off, size)] if m == 0 else rows.at[pl.ds(m * BLOCK + off, size)]
+        src = emb.at[pl.ds(*ROW_THIRDS[j])] if m == 0 else rows.at[row_at(m, 0, j)]
+        dst = rows.at[row_at(n, 0, j)]
         return remote(src, dst, row_send.at[n, j], row_recv.at[n, j], row_peer(1 << d))
 
     def cent_copy(d, j, m):
-        off, size = CENT_THIRDS[j]
         n = m | 1 << d
-        src = cents.at[pl.ds(PLACE[m] * CENTS + off, size)]
-        dst = cents.at[pl.ds(PLACE[n] * CENTS + off, size)]
+        src, dst = cents.at[cent_at(m, j)], cents.at[cent_at(n, j)]
         return remote(src, dst, cent_send.at[n, j], cent_recv.at[n, j], cent_peer(1 << d))
 
     def sib_copy(n, j):
-        off, size = ROW_THIRDS[j]
-        src = emb.at[pl.ds(off, size)] if n == 0 else rows.at[pl.ds(n * BLOCK + off, size)]
-        dst = rows.at[pl.ds(n * BLOCK + ROWS + off, size)]
+        src = emb.at[pl.ds(*ROW_THIRDS[j])] if n == 0 else rows.at[row_at(n, 0, j)]
+        dst = rows.at[row_at(n, 1, j)]
         return remote(src, dst, sib_send.at[n, j], sib_recv.at[n, j], row_peer(0, 1))
 
     wave = waves()
@@ -134,34 +139,33 @@
             total = jnp.sum(c * c, axis=1, keepdims=True) * (0.5 * ALPHA)
             half_sq[at, :] = jnp.broadcast_to(total, (CENTS, 128))
 
-    def score(n, half):
-        if half == 0:
-            peak[n] = jnp.full((8, BLOCK), -jnp.inf, jnp.float32)
-
-        @pl.loop(0, 2)
-        def _(i):
+    def score(p, half):
+        cols = pl.ds(pl.multiple_of(p * BLOCK, BLOCK), BLOCK)
+        top = jnp.where(half == 0, -jnp.inf, peak[p])
+        for i in range(2):
             at = pl.ds(pl.multiple_of(half * 512 + i * 256, 256), 256)
             product = lax.dot_general(
-                cents[at, :], rows[n * BLOCK : (n + 1) * BLOCK, :], NT,
-                preferred_element_type=jnp.float32,
+                cents[at, :], rows[cols, :], NT, preferred_element_type=jnp.float32
             )
             h = half_sq[at, :]
             t = product * ALPHA - jnp.concatenate([h] * (BLOCK // 128), axis=1)
-            scores[at, n * BLOCK : (n + 1) * BLOCK] = t
-            peak[n] = jnp.maximum(peak[n], jnp.max(t.reshape(32, 8, BLOCK), axis=0))
-
-    def soften(n):
-        top = jnp.max(peak[n], axis=0, keepdims=True)
-
-        def body(i, total):
-            at = pl.ds(pl.multiple_of(i * 256, 256), 256)
-            e = jnp.exp2(scores[at, n * BLOCK : (n + 1) * BLOCK] - top)
-            return total + jnp.sum(e.reshape(32, 8, BLOCK), axis=0)
-
-        total = lax.fori_loop(0, 4, body, jnp.zeros((8, BLOCK), jnp.float32))
+            scores[at, cols] = t
+            top = jnp.maximum(top, jnp.max(t.reshape(32, 8, BLOCK), axis=0))
+        peak[p] = top
+
+    def soften(p):
+        cols = pl.ds(pl.multiple_of(p * BLOCK, BLOCK), BLOCK)
+        top = jnp.max(peak[p], axis=0, keepdims=True)
+        total = jnp.zeros((8, BLOCK), jnp.float32)
+        for i in range(4):
+            e = jnp.exp2(scores[i * 256 : (i + 1) * 256, cols] - top)
+            total = total + jnp.sum(e.reshape(32, 8, BLOCK), axis=0)
         lse = top + jnp.log2(jnp.sum(total, axis=0, keepdims=True))
-        lse_mine[2 * n] = lse[:, :ROWS]
-        lse_mine[2 * n + 1] = lse[:, ROWS:]
+        lse_mine[2 * p] = lse[:, :ROWS]
+        lse_mine[2 * p + 1] = lse[:, ROWS:]
+
+    def mirror(s, a):
+        return 2 * PLACE[ORDER[s // 2] ^ ORDER[a // 2]] + (s % 2 ^ a % 2)
 
     def stat_copy(a):
         return remote(lse_mine.at[a], lse_in.at[a], stat_send.at[a], stat_recv, slot_peer(a))
@@ -175,7 +179,9 @@
         )
 
     def count_copy(n):
-        return remote(count_mine.at[n], count_in.at[n], count_send.at[n], count_recv, cent_peer(n))
+        return remote(
+            count_mine.at[n], count_in.at[n], count_send.at[n], count_recv, cent_peer(ORDER[n])
+        )
 
     def wait_all(ref, sem):
         remote(ref, ref, own_sem, sem, row_peer(0, 1)).wait_recv()
@@ -198,55 +204,61 @@
     cent_start(5)
     cent_arrive(2)
     own.wait()
-    sib_arrive(0)
     squares(0)
-    score(0, 0)
-    row_arrive(1)
-    row_start(5)
-    cent_arrive(3)
-    cent_start(6)
-    row_arrive(2)
-    for n in (1, 2, 4):
-        sib_arrive(n)
-        score(n, 0)
-    cent_arrive(4)
-    cent_arrive(5)
-    cent_arrive(6)
-    squares(1)
-
-    def finish(n):
-        score(n, 1)
-        soften(n)
-        if n < 6:
-            for a in (2 * n, 2 * n + 1):
-                if a:
-                    stat_copy(a).start()
-
-    finish(0)
-    row_arrive(3)
-    row_start(6)
-    finish(1)
-    finish(2)
-    row_arrive(4)
-    finish(4)
-    row_arrive(5)
-    for n in (3, 5):
-        sib_arrive(n)
-        score(n, 0)
-        finish(n)
-    sib_arrive(6)
-    score(6, 0)
-    finish(6)
-    row_arrive(6)
-    sib_arrive(7)
-    score(7, 0)
-    score(7, 1)
-    wait_all(lse_in.at[pl.ds(1, 11)], stat_recv)
-    part = combine([lse_mine[0]] + [lse_in[a] for a in range(1, 12)])
-    part_mine[...] = part
-    for a in range(1, 16):
-        part_copy(a).start()
-    soften(7)
+
+    def before(t):
+        if t == 0:
+            sib_arrive(0)
+        if t == 1:
+            row_arrive(1)
+            row_start(5)
+            cent_arrive(3)
+            cent_start(6)
+            row_arrive(2)
+        if t in (1, 2, 3):
+            sib_arrive(ORDER[t])
+        if t == 4:
+            for w in (4, 5, 6):
+                cent_arrive(w)
+            squares(1)
+        if t == 5:
+            row_arrive(3)
+            row_start(6)
+        if t == 7:
+            row_arrive(4)
+        if t == 8:
+            row_arrive(5)
+        if t == 12:
+            row_arrive(6)
+        if t in (8, 10, 12, 14):
+            sib_arrive(ORDER[t // 2])
+
+    @pl.loop(0, 16)
+    def _(t):
+        for when in (0, 1, 2, 3, 4, 5, 7, 8, 10, 12, 14):
+            pl.when(t == when)(functools.partial(before, when))
+        p = jnp.where(t < 8, t % 4, t // 2)
+        half = jnp.where(t < 8, t // 4, t % 2)
+        score(p, half)
+
+        @pl.when(t == 15)
+        def _():
+            wait_all(lse_in.at[pl.ds(1, 11)], stat_recv)
+            part_mine[...] = combine([lse_mine[0]] + [lse_in[a] for a in range(1, 12)])
+            for a in range(1, 16):
+                part_copy(a).start()
+
+        @pl.when(half == 1)
+        def _():
+            soften(p)
+            for q in range(6):
+
+                @pl.when(p == q)
+                def _():
+                    for a in (2 * q, 2 * q + 1):
+                        if a:
+                            stat_copy(a).start()
+
     for a in range(1, 16):
         fin_copy(a).start()
     wait_all(part_in.at[pl.ds(1, 15)], part_recv)
@@ -254,75 +266,81 @@
     for s in range(16):
         terms = [part_mine[...] if s == 0 else part_in[s]]
         for q in range(12, 16):
-            terms.append(lse_mine[q] if s == q else fin_in[s ^ q, q - 12])
+            a = mirror(s, q)
+            terms.append(lse_mine[q] if a == 0 else fin_in[a, q - 12])
         lse = combine(terms)
         lse_all[:, s * ROWS : (s + 1) * ROWS] = lse
         if s == 0:
-            norm_out[...] = lse * LN2
-
-    def weigh(n):
-        at = PLACE[n] * CENTS
-        sums[n] = jnp.zeros((CENTS, WIDTH), jnp.float32)
-        tally[...] = jnp.zeros((CENTS, 128), jnp.float32)
-
-        @pl.loop(0, 8)
-        def _(r):
-            cols = pl.ds(pl.multiple_of(r * BLOCK, BLOCK), BLOCK)
-            resp = jnp.exp2(scores[at : at + CENTS, cols] - lse_all[:, cols]).astype(jnp.bfloat16)
+            norm_out[...] = (lse * LN2).reshape(ROWS)
+
+    def weigh(p):
+        at = pl.ds(pl.multiple_of(p * CENTS, CENTS), CENTS)
+        count = jnp.zeros((CENTS, 128), jnp.float32)
+        total = jnp.zeros((CENTS, WIDTH), jnp.float32)
+        for r in range(8):
+            cols = slice(r * BLOCK, (r + 1) * BLOCK)
+            resp = jnp.exp2(scores[at, cols] - lse_all[:, cols]).astype(jnp.bfloat16)
             wide = resp.astype(jnp.float32)
-            tally[...] += functools.reduce(
-                jnp.add, [wide[:, q * 128 : (q + 1) * 128] for q in range(BLOCK // 128)]
+            for q in range(BLOCK // 128):
+                count = count + wide[:, q * 128 : (q + 1) * 128]
+            total = total + lax.dot_general(
+                resp, rows[cols, :], NN, preferred_element_type=jnp.float32
             )
-            sums[n] += lax.dot_general(resp, rows[cols, :], NN, preferred_element_type=jnp.float32)
-
-        count_mine[n] = jnp.sum(tally[...].T, axis=0, keepdims=True)
-        if n:
-            count_copy(n).start()
+        sums[p] = total
+        outbox[p] = total.astype(jnp.bfloat16)
+        count_mine[p] = jnp.sum(count.T, axis=0, keepdims=True)
 
     def step_of(n, j):
         return next(s for s in range(3) if n >> (j + s) % 3 & 1)
 
     def sum_copy(n, j):
-        off, size = CENT_THIRDS[j]
+        at = pl.ds(*CENT_THIRDS[j])
         s = step_of(n, j)
         d = (j + s) % 3
-        to = n ^ 1 << d
         box = (inbox1, inbox2, inbox3)[s]
-        dst = box.at[0 if s == 2 else to, pl.ds(off, size)]
+        dst = box.at[0 if s == 2 else PLACE[n ^ 1 << d], at]
         return remote(
-            outbox.at[n, pl.ds(off, size)], dst, sum_send.at[n, j], sum_recv.at[n, j],
-            cent_peer(1 << d),
+            outbox.at[PLACE[n], at], dst, sum_send.at[n, j], sum_recv.at[n, j], cent_peer(1 << d)
         )
 
     def gathered(n, j):
         off, size = CENT_THIRDS[j]
-        value = sums[n, off : off + size, :]
+        value = sums[PLACE[n], off : off + size, :]
         for s in range(step_of(n, j) if n else 3):
             came = n | 1 << (j + s) % 3
             sum_copy(came, j).wait_recv()
             box = (inbox1, inbox2, inbox3)[s]
-            value = value + box[0 if s == 2 else n, off : off + size, :].astype(jnp.float32)
+            at = 0 if s == 2 else PLACE[n]
+            value = value + box[at, off : off + size, :].astype(jnp.float32)
         return value
 
     def send_sums(n, step):
         for j in range(3):
             if step_of(n, j) == step:
-                off, size = CENT_THIRDS[j]
-                outbox[n, off : off + size, :] = gathered(n, j).astype(jnp.bfloat16)
+                if step:
+                    off, size = CENT_THIRDS[j]
+                    outbox[PLACE[n], off : off + size, :] = gathered(n, j).astype(jnp.bfloat16)
                 sum_copy(n, j).start()
 
-    for n in (7, 3, 6, 5):
-        weigh(n)
-        send_sums(n, 0)
-    for n in (3, 6, 5):
-        send_sums(n, 1)
-    for n in (1, 2, 4):
-        weigh(n)
-        send_sums(n, 0)
-    for n in (1, 2, 4):
-        send_sums(n, 1)
-    weigh(0)
-    for n in (1, 2, 4):
+    def after(p):
+        n = ORDER[p]
+        if n:
+            send_sums(n, 0)
+            count_copy(p).start()
+        if p == 4:
+            for m in (6, 5, 3):
+                send_sums(m, 1)
+        if p == 1:
+            for m in (4, 2, 1):
+                send_sums(m, 1)
+
+    @pl.loop(0, 8)
+    def _(i):
+        weigh(7 - i)
+        for p in range(8):
+            pl.when(i == 7 - p)(functools.partial(after, p))
+
+    for n in (4, 2, 1):
         send_sums(n, 2)
 
     for w in range(7):
@@ -339,7 +357,7 @@
         fin_copy(a).wait_send()
     wait_all(count_in.at[pl.ds(1, 7)], count_recv)
     count = functools.reduce(jnp.add, [count_mine[0]] + [count_in[n] for n in range(1, 8)])
-    count_out[...] = count
+    count_out[...] = count.reshape(CENTS)
     below = jnp.broadcast_to(count, (CENTS, 128)).T + PRIOR
     for j in range(3):
         off, size = CENT_THIRDS[j]
@@ -353,6 +371,24 @@
             sum_copy(n, j).wait_send()
 
 
+def hand_over(*results):
+    def body(*refs):
+        ins, outs, sems = refs[:3], refs[3:6], refs[6]
+        copies = [pltpu.make_async_copy(a, b, sems.at[i]) for i, (a, b) in enumerate(zip(ins, outs))]
+        for copy in copies:
+            copy.start()
+        for copy in copies:
+            copy.wait()
+
+    return pl.pallas_call(
+        body,
+        out_shape=[jax.ShapeDtypeStruct(r.shape, r.dtype) for r in results],
+        in_specs=[pl.BlockSpec(memory_space=pl.ANY)] * 3,
+        out_specs=[pl.BlockSpec(memory_space=pl.ANY)] * 3,
+        scratch_shapes=[pltpu.SemaphoreType.DMA((3,))],
+    )(*results)
+
+
 def local(embeddings, codebook):
     f32, bf16 = jnp.float32, jnp.bfloat16
     vmem, dma = pltpu.VMEM, pltpu.SemaphoreType.DMA
@@ -360,8 +396,8 @@
         kernel,
         out_shape=(
             jax.ShapeDtypeStruct((CENTS, WIDTH), f32),
-            jax.ShapeDtypeStruct((1, CENTS), f32),
-            jax.ShapeDtypeStruct((1, ROWS), f32),
+            jax.ShapeDtypeStruct((CENTS,), f32),
+            jax.ShapeDtypeStruct((ROWS,), f32),
         ),
         in_specs=[pl.BlockSpec(memory_space=pl.ANY), pl.BlockSpec(memory_space=pltpu.VMEM)],
         out_specs=[pl.BlockSpec(memory_space=pltpu.VMEM)] * 3,
@@ -402,7 +438,7 @@
             flops=4 * 4096 * 1024 * 1024, bytes_accessed=2**21, transcendentals=2**23
         ),
     )(embeddings, codebook)
-    return new, count.reshape(CENTS), norm.reshape(ROWS)
+    return hand_over(new, count, norm)
 
 
 def solution(mesh):

time: 83.3 us -> 84.9 us (1.019)
  Pallas kernels: 79.4 us -> 84 us
  local copies, waits for them, and re-layouts: 3.08 us -> 0 us
    pallas_call x0 -> x1, Pallas kernels: none -> 17.1 us  [hand_over(): pl.pallas_call(body, out_shape=[jax.ShapeDtypeStruct(r.shape, r.dtype) fo...]
    pallas_call x1, Pallas kernels: 79.4 us -> 67 us  [local(): pl.pallas_call(kernel, out_shape=(jax.ShapeDtypeStruct((CENTS, WIDTH), f3...]
    unnamed x7 -> x0, local copies, waits for them, and re-layouts: 3.08 us -> none
where the time goes in v2:
time: 84.9 us; the launch traced here: 84.7 us
  Pallas kernels  84 us (99%)
    pallas_call x1, Pallas kernels, local(): pl.pallas_call(kernel, out_shape=(jax.ShapeDtypeStruct((CENTS, WIDTH), f3...  67 us
    pallas_call x1, Pallas kernels, hand_over(): pl.pallas_call(body, out_shape=[jax.ShapeDtypeStruct(r.shape, r.dtype) fo...  17.1 us

profile of v2, /device:TPU:1, one launch (start us, length us, event | category | flops | bytes accessed | tf_op | source)
XLA Modules:
  0.0 84.7 jit_solution(6409248429569869447)
XLA Ops:
  0.6 67.0 %shard_map.49 = (f32[128,1024]{1,0:T(8,128)}, f32[128]{0:T(128)}, f32[256]{0:T(256)}) custom-call(bf16[256,1024]{1,0:T(8,128)(2,1)} %emb.1, f32[128,1024]{1,0:T(8,128)} %book.1), custom_call_target="tpu_custom_call" | custom-call | flops 17179869184 | bytes 2097152 | tf_op jit(solution)/shard_map/pallas_call | solution.py:395
  67.6 17.1 %shard_map.50 = (f32[128,1024]{1,0:T(8,128)}, f32[128]{0:T(128)}, f32[256]{0:T(256)}) custom-call(f32[128,1024]{1,0:T(8,128)} %get-tuple-element.6.refs_0_, f32[128]{0:T(128)} %get-tuple-element.7.refs_1_, f32[256]{0:T(256)} %get-tuple-element.8.refs_2_), custom_call_target="tpu_custom_call" | custom-call | tf_op jit(solution)/shard_map/pallas_call | solution.py:383

commit v3 on v2

--- a/solution.py
+++ b/solution.py
@@ -373,19 +373,14 @@
 
 def hand_over(*results):
     def body(*refs):
-        ins, outs, sems = refs[:3], refs[3:6], refs[6]
-        copies = [pltpu.make_async_copy(a, b, sems.at[i]) for i, (a, b) in enumerate(zip(ins, outs))]
-        for copy in copies:
-            copy.start()
-        for copy in copies:
-            copy.wait()
+        for i in range(3):
+            refs[3 + i][...] = refs[i][...]
 
     return pl.pallas_call(
         body,
         out_shape=[jax.ShapeDtypeStruct(r.shape, r.dtype) for r in results],
-        in_specs=[pl.BlockSpec(memory_space=pl.ANY)] * 3,
-        out_specs=[pl.BlockSpec(memory_space=pl.ANY)] * 3,
-        scratch_shapes=[pltpu.SemaphoreType.DMA((3,))],
+        in_specs=[pl.BlockSpec(memory_space=pltpu.VMEM)] * 3,
+        out_specs=[pl.BlockSpec(memory_space=pltpu.VMEM)] * 3,
     )(*results)
 
 

time: 84.9 us -> 69.7 us (0.82)
  Pallas kernels: 84 us -> 68.8 us
    pallas_call x1, Pallas kernels: 17.1 us -> 1.88 us  [hand_over(): pl.pallas_call(body, out_shape=[jax.ShapeDtypeStruct(r.shape, r.dtype) fo...]
where the time goes in v3:
time: 69.7 us; the launch traced here: 69.5 us
  Pallas kernels  68.8 us (99%)
    pallas_call x1, Pallas kernels, local(): pl.pallas_call(kernel, out_shape=(jax.ShapeDtypeStruct((CENTS, WIDTH), f3...  67 us
    pallas_call x1, Pallas kernels, hand_over(): pl.pallas_call(body, out_shape=[jax.ShapeDtypeStruct(r.shape, r.dtype) fo...  1.88 us

profile of v3, /device:TPU:1, one launch (start us, length us, event | category | flops | bytes accessed | tf_op | source)
XLA Modules:
  0.0 69.5 jit_solution(18073247124080711846)
XLA Ops:
  0.6 67.0 %shard_map.49 = (f32[128,1024]{1,0:T(8,128)}, f32[128]{0:T(128)}, f32[256]{0:T(256)}) custom-call(bf16[256,1024]{1,0:T(8,128)(2,1)} %emb.1, f32[128,1024]{1,0:T(8,128)} %book.1), custom_call_target="tpu_custom_call" | custom-call | flops 17179869184 | bytes 2097152 | tf_op jit(solution)/shard_map/pallas_call | solution.py:390
  67.6 1.9 %shard_map.50 = (f32[128,1024]{1,0:T(8,128)}, f32[128]{0:T(128)}, f32[256]{0:T(256)}) custom-call(f32[128,1024]{1,0:T(8,128)} %get-tuple-element.6.refs_0_, f32[128]{0:T(128)} %get-tuple-element.7.refs_1_, f32[256]{0:T(256)} %get-tuple-element.8.refs_2_), custom_call_target="tpu_custom_call" | custom-call | tf_op jit(solution)/shard_map/pallas_call | solution.py:379

commit v4 on v3

v4 whole, which is shorter than its diff:
```python
import functools
import math

import jax
import jax.numpy as jnp
from jax import lax
from jax.experimental import pallas as pl
from jax.experimental.pallas import tpu as pltpu
from jax.sharding import PartitionSpec as P

TEMPER = 0.8
PRIOR = 1.0
ALPHA = math.log2(math.e) / TEMPER
LN2 = math.log(2.0)
MESH = pl.DeviceIdType.MESH

ROWS, CENTS, WIDTH = 256, 128, 1024
PART, UNIT = 128, 256
PIECES = (
    (0, 16, (2, 1, 0)),
    (16, 32, (1, 2, 0)),
    (48, 16, (2, 0, 1)),
    (64, 32, (0, 2, 1)),
    (96, 16, (1, 0, 2)),
    (112, 16, (0, 1, 2)),
)
N_PIECES = len(PIECES)
ORDER = (0, 1, 2, 4, 3, 5, 6, 7)
PLACE = {mask: i for i, mask in enumerate(ORDER)}
NT = (((1,), (1,)), ((), ()))
NN = (((1,), (0,)), ((), ()))


def waves():
    wave = [[] for _ in range(7)]
    for j, (_, _, (a, b, c)) in enumerate(PIECES):
        sent = ((a, 0), (b, 0), (c, 0), (b, 1 << a), (c, 1 << a), (c, 1 << b), (c, 1 << a | 1 << b))
        for w, (d, m) in enumerate(sent):
            wave[w].append((d, j, m))
    return wave


def combine(terms):
    top = functools.reduce(jnp.maximum, terms)
    total = functools.reduce(jnp.add, [jnp.exp2(t - top) for t in terms])
    return top + jnp.log2(total)


def kernel(
    emb, book, new_out, count_out, norm_out,
    rows, cents, scores, half_sq, peak, sums, tally, lse_all,
    lse_mine, lse_in, part_mine, part_in, fin_in, count_mine, count_in,
    outbox, inbox1, inbox2, inbox3,
    book_in, own_sem, row_send, row_recv, sib_send, sib_recv, cent_send, cent_recv,
    stat_send, stat_recv, part_send, part_recv, fin_send, fin_recv,
    count_send, count_recv, sum_send, sum_recv,
):
    dp, cent = lax.axis_index("dp"), lax.axis_index("cent")
    place = (cent // 4, cent % 4, dp // 2)
    core = dp % 2

    def device(p, c):
        return (p[2] * 2 + c, p[0] * 4 + p[1])

    def row_peer(mask, other=0):
        p = [v + 1 - 2 * (v % 2) if mask >> d & 1 else v for d, v in enumerate(place)]
        return device(p, 1 - core if other else core)

    def cent_peer(mask):
        return device([3 - v if mask >> d & 1 else v for d, v in enumerate(place)], core)

    def slot_peer(a):
        return row_peer(ORDER[a // 2], a % 2)

    def remote(src, dst, send, recv, to):
        return pltpu.make_async_remote_copy(
            src_ref=src, dst_ref=dst, send_sem=send, recv_sem=recv,
            device_id=to, device_id_type=MESH,
        )

    barrier = pltpu.get_barrier_semaphore()
    peers = [row_peer(0, 1)] + [row_peer(b) for b in (1, 2, 4)] + [cent_peer(b) for b in (1, 2, 4)]
    for peer in peers:
        pl.semaphore_signal(barrier, inc=1, device_id=peer, device_id_type=MESH)
    own = [
        pltpu.make_async_copy(
            emb.at[pl.ds(r * PART, PART)], rows.at[pl.ds(r * 8 * UNIT, PART)], own_sem.at[r]
        )
        for r in range(2)
    ]
    own.append(pltpu.make_async_copy(book, book_in, own_sem.at[2]))
    own[2].start()
    own[0].start()
    own[1].start()
    pl.semaphore_wait(barrier, len(peers))

    def row_at(r, n, k, j):
        return pl.ds((r * 8 + PLACE[n]) * UNIT + k * PART + PIECES[j][0], PIECES[j][1])

    def cent_at(n, j):
        return pl.ds(PLACE[n] * CENTS + PIECES[j][0], PIECES[j][1])

    def row_source(r, m, j):
        if m == 0:
            return emb.at[pl.ds(r * PART + PIECES[j][0], PIECES[j][1])]
        return rows.at[row_at(r, m, 0, j)]

    def row_copy(r, d, j, m):
        n = m | 1 << d
        return remote(
            row_source(r, m, j), rows.at[row_at(r, n, 0, j)],
            row_send.at[r, n, j], row_recv.at[r, n, j], row_peer(1 << d),
        )

    def cent_copy(d, j, m):
        n = m | 1 << d
        src, dst = cents.at[cent_at(m, j)], cents.at[cent_at(n, j)]
        return remote(src, dst, cent_send.at[n, j], cent_recv.at[n, j], cent_peer(1 << d))

    def sib_copy(r, n, j):
        return remote(
            row_source(r, n, j), rows.at[row_at(r, n, 1, j)],
            sib_send.at[r, n, j], sib_recv.at[r, n, j], row_peer(0, 1),
        )

    wave = waves()

    def row_start(r, w):
        for msg in wave[w]:
            row_copy(r, *msg).start()

    def cent_start(w):
        for msg in wave[w]:
            cent_copy(*msg).start()

    def row_arrive(r, w):
        for d, j, m in wave[w]:
            row_copy(r, d, j, m).wait_recv()
            sib_copy(r, m | 1 << d, j).start()

    def cent_arrive(w):
        for msg in wave[w]:
            cent_copy(*msg).wait_recv()

    def sib_arrive(r, p):
        for j in range(N_PIECES):
            sib_copy(r, ORDER[p], j).wait_recv()

    def squares(half):
        @pl.loop(0, 4)
        def _(i):
            at = pl.ds(pl.multiple_of(half * 512 + i * CENTS, CENTS), CENTS)
            c = cents[at, :].astype(jnp.float32)
            total = jnp.sum(c * c, axis=1, keepdims=True) * (0.5 * ALPHA)
            half_sq[at, :] = jnp.broadcast_to(total, (CENTS, 128))

    def columns(u):
        return pl.ds(pl.multiple_of(u * UNIT, UNIT), UNIT)

    def score(u, blocks, fresh, last=None):
        cols = columns(u)
        top = jnp.full((8, UNIT), -jnp.inf, jnp.float32) if fresh else peak[u]
        if last is not None:
            summed = columns(last)
            high = jnp.max(peak[last], axis=0, keepdims=True)
            total = jnp.zeros((8, UNIT), jnp.float32)
        for i in blocks:
            at = slice(i * 256, (i + 1) * 256)
            product = lax.dot_general(
                cents[at, :], rows[cols, :], NT, preferred_element_type=jnp.float32
            )
            if last is not None:
                step = 1024 // len(blocks)
                first = (i - blocks[0]) * step
                e = jnp.exp2(scores[first : first + step, summed] - high)
                total = total + jnp.sum(e.reshape(step // 8, 8, UNIT), axis=0)
            h = half_sq[at, :]
            t = product * ALPHA - jnp.concatenate([h] * (UNIT // 128), axis=1)
            scores[at, cols] = t
            top = jnp.maximum(top, jnp.max(t.reshape(32, 8, UNIT), axis=0))
        peak[u] = top
        if last is not None:
            settle(last, high, total)

    def settle(u, high, total):
        lse = high + jnp.log2(jnp.sum(total, axis=0, keepdims=True))
        r, p = u // 8, u % 8
        lse_mine[r, 2 * p] = lse[:, :PART]
        lse_mine[r, 2 * p + 1] = lse[:, PART:]

    def soften(u):
        high = jnp.max(peak[u], axis=0, keepdims=True)
        total = jnp.zeros((8, UNIT), jnp.float32)
        for i in range(4):
            e = jnp.exp2(scores[i * 256 : (i + 1) * 256, columns(u)] - high)
            total = total + jnp.sum(e.reshape(32, 8, UNIT), axis=0)
        settle(u, high, total)

    def mirror(s, a):
        return 2 * PLACE[ORDER[s // 2] ^ ORDER[a // 2]] + (s % 2 ^ a % 2)

    def stat_copy(r, a):
        return remote(
            lse_mine.at[r, a], lse_in.at[r, a], stat_send.at[r, a], stat_recv.at[r], slot_peer(a)
        )

    def part_copy(r, a):
        return remote(
            part_mine.at[r], part_in.at[r, a], part_send.at[r, a], part_recv.at[r], slot_peer(a)
        )

    def fin_copy(r, a):
        return remote(
            lse_mine.at[r, pl.ds(12, 4)], fin_in.at[r, a],
            fin_send.at[r, a], fin_recv.at[r], slot_peer(a),
        )

    def count_copy(n):
        return remote(
            count_mine.at[n], count_in.at[n], count_send.at[n], count_recv, cent_peer(ORDER[n])
        )

    def wait_all(ref, sem):
        remote(ref, ref, own_sem.at[0], sem, row_peer(0, 1)).wait_recv()

    def settled(u):
        r, p = u // 8, u % 8
        if p < 6:
            for a in (2 * p, 2 * p + 1):
                if a:
                    stat_copy(r, a).start()
        if p == 6:
            wait_all(lse_in.at[r, pl.ds(1, 11)], stat_recv.at[r])
            part_mine[r] = combine([lse_mine[r, 0]] + [lse_in[r, a] for a in range(1, 12)])
            for a in range(1, 16):
                part_copy(r, a).start()
        if p == 7:
            for a in range(1, 16):
                fin_copy(r, a).start()

    def agree(r):
        wait_all(part_in.at[r, pl.ds(1, 15)], part_recv.at[r])
        wait_all(fin_in.at[r, pl.ds(1, 15)], fin_recv.at[r])
        for s in range(16):
            terms = [part_mine[r] if s == 0 else part_in[r, s]]
            for q in range(12, 16):
                a = mirror(s, q)
                terms.append(lse_mine[r, q] if a == 0 else fin_in[r, a, q - 12])
            lse = combine(terms)
            at = (r * 16 + s) * PART
            lse_all[:, at : at + PART] = lse
            if s == 0:
                norm_out[r * PART : (r + 1) * PART] = (lse * LN2).reshape(PART)

    for w in range(3):
        row_start(0, w)
    own[2].wait()
    cents[0:CENTS, :] = book_in[...].astype(jnp.bfloat16)
    for w in range(3):
        cent_start(w)
    for r in range(2):
        for j in range(N_PIECES):
            sib_copy(r, 0, j).start()
    own[0].wait()
    own[1].wait()
    cent_arrive(0)
    cent_start(3)
    cent_start(4)
    row_arrive(0, 0)
    row_start(0, 3)
    row_start(0, 4)
    cent_arrive(1)
    cent_start(5)
    row_arrive(0, 1)
    row_start(0, 5)
    cent_arrive(2)
    squares(0)
    row_arrive(0, 2)
    cent_arrive(3)
    cent_start(6)
    row_arrive(0, 3)
    row_start(0, 6)
    row_start(1, 0)
    for p in range(4):
        sib_arrive(0, p)

    @pl.loop(0, 4)
    def _(u):
        score(u, (0, 1), True)

    row_arrive(0, 4)
    cent_arrive(4)
    row_arrive(0, 5)
    row_start(1, 1)
    row_start(1, 2)
    cent_arrive(5)
    row_arrive(0, 6)
    cent_arrive(6)
    squares(1)
    score(0, (2, 3), False)

    @pl.loop(1, 4)
    def _(u):
        @pl.when(u == 2)
        def _():
            row_arrive(1, 0)
            row_start(1, 3)
            row_start(1, 4)

        score(u, (2, 3), False, u - 1)
        for v in range(3):
            pl.when(u == v + 1)(functools.partial(settled, v))

    def before(u):
        if u == 5:
            row_arrive(1, 1)
            row_start(1, 5)
        if u == 8:
            row_arrive(1, 2)
        if u == 10:
            row_arrive(1, 3)
            row_start(1, 6)
        if u == 14:
            row_arrive(1, 6)
        sib_arrive(u // 8, u % 8)

    def unit_loop(lo, hi):
        @pl.loop(lo, hi)
        def _(u):
            for v in range(lo, hi):
                pl.when(u == v)(functools.partial(before, v))
            score(u, (0, 1, 2, 3), True, u - 1)
            for v in range(lo, hi):
                pl.when(u == v)(functools.partial(settled, v - 1))

    def weigh(p, r):
        at = pl.ds(pl.multiple_of(p * CENTS, CENTS), CENTS)
        count = tally[p] if r else jnp.zeros((CENTS, 128), jnp.float32)
        total = sums[p] if r else jnp.zeros((CENTS, WIDTH), jnp.float32)
        for i in range(4):
            cols = slice((r * 4 + i) * 2 * UNIT, (r * 4 + i + 1) * 2 * UNIT)
            resp = jnp.exp2(scores[at, cols] - lse_all[:, cols]).astype(jnp.bfloat16)
            wide = resp.astype(jnp.float32)
            for q in range(2 * UNIT // 128):
                count = count + wide[:, q * 128 : (q + 1) * 128]
            total = total + lax.dot_general(
                resp, rows[cols, :], NN, preferred_element_type=jnp.float32
            )
        sums[p] = total
        if r:
            outbox[p] = total.astype(jnp.bfloat16)
            count_mine[p] = jnp.sum(count.T, axis=0, keepdims=True)
        else:
            tally[p] = count

    def step_of(n, j):
        return next(s for s in range(3) if n >> PIECES[j][2][s] & 1)

    def sum_copy(n, j):
        at = pl.ds(*PIECES[j][:2])
        s = step_of(n, j)
        d = PIECES[j][2][s]
        box = (inbox1, inbox2, inbox3)[s]
        dst = box.at[0 if s == 2 else PLACE[n ^ 1 << d], at]
        return remote(
            outbox.at[PLACE[n], at], dst, sum_send.at[n, j], sum_recv.at[n, j], cent_peer(1 << d)
        )

    def gathered(n, j):
        off, size, order = PIECES[j]
        value = sums[PLACE[n], off : off + size, :]
        for s in range(step_of(n, j) if n else 3):
            came = n | 1 << order[s]
            sum_copy(came, j).wait_recv()
            box = (inbox1, inbox2, inbox3)[s]
            at = 0 if s == 2 else PLACE[n]
            value = value + box[at, off : off + size, :].astype(jnp.float32)
        return value

    def send_sums(n, step):
        for j in range(N_PIECES):
            if step_of(n, j) == step:
                if step:
                    off, size, _ = PIECES[j]
                    outbox[PLACE[n], off : off + size, :] = gathered(n, j).astype(jnp.bfloat16)
                sum_copy(n, j).start()

    def after(p):
        n = ORDER[p]
        if n:
            send_sums(n, 0)
            count_copy(p).start()
        if p == 4:
            for m in (6, 5, 3):
                send_sums(m, 1)
        if p == 1:
            for m in (4, 2, 1):
                send_sums(m, 1)

    unit_loop(4, 12)
    agree(0)

    @pl.loop(0, 3)
    def _(i):
        weigh(7 - i, 0)
        pl.when(i == 0)(functools.partial(row_arrive, 1, 4))

    row_arrive(1, 5)
    unit_loop(12, 16)
    soften(15)
    settled(15)

    @pl.loop(3, 8)
    def _(i):
        weigh(7 - i, 0)

    agree(1)

    @pl.loop(0, 8)
    def _(i):
        weigh(7 - i, 1)
        for p in range(8):
            pl.when(i == 7 - p)(functools.partial(after, p))

    for n in (4, 2, 1):
        send_sums(n, 2)

    for w in range(7):
        for msg in wave[w]:
            row_copy(0, *msg).wait_send()
            row_copy(1, *msg).wait_send()
            cent_copy(*msg).wait_send()
    for r in range(2):
        for n in range(8):
            for j in range(N_PIECES):
                sib_copy(r, n, j).wait_send()
        for a in range(1, 16):
            if a < 12:
                stat_copy(r, a).wait_send()
            part_copy(r, a).wait_send()
            fin_copy(r, a).wait_send()
    wait_all(count_in.at[pl.ds(1, 7)], count_recv)
    count = functools.reduce(jnp.add, [count_mine[0]] + [count_in[n] for n in range(1, 8)])
    count_out[...] = count.reshape(CENTS)
    below = jnp.broadcast_to(count, (CENTS, 128)).T + PRIOR
    for j in range(N_PIECES):
        off, size, _ = PIECES[j]
        top = gathered(0, j) + PRIOR * book_in[off : off + size, :]
        for q in range(WIDTH // 128):
            cols = slice(q * 128, (q + 1) * 128)
            new_out[off : off + size, cols] = top[:, cols] / below[off : off + size, :]
    for n in range(1, 8):
        count_copy(n).wait_send()
        for j in range(N_PIECES):
            sum_copy(n, j).wait_send()


def hand_over(*results):
    def body(*refs):
        for i in range(3):
            refs[3 + i][...] = refs[i][...]

    return pl.pallas_call(
        body,
        out_shape=[jax.ShapeDtypeStruct(r.shape, r.dtype) for r in results],
        in_specs=[pl.BlockSpec(memory_space=pltpu.VMEM)] * 3,
        out_specs=[pl.BlockSpec(memory_space=pltpu.VMEM)] * 3,
    )(*results)


def local(embeddings, codebook):
    f32, bf16 = jnp.float32, jnp.bfloat16
    vmem, dma = pltpu.VMEM, pltpu.SemaphoreType.DMA
    new, count, norm = pl.pallas_call(
        kernel,
        out_shape=(
            jax.ShapeDtypeStruct((CENTS, WIDTH), f32),
            jax.ShapeDtypeStruct((CENTS,), f32),
            jax.ShapeDtypeStruct((ROWS,), f32),
        ),
        in_specs=[pl.BlockSpec(memory_space=pl.ANY)] * 2,
        out_specs=[pl.BlockSpec(memory_space=pltpu.VMEM)] * 3,
        scratch_shapes=[
            vmem((16 * UNIT, WIDTH), bf16),
            vmem((8 * CENTS, WIDTH), bf16),
            vmem((8 * CENTS, 16 * UNIT), f32),
            vmem((8 * CENTS, 128), f32),
            vmem((16, 8, UNIT), f32),
            vmem((8, CENTS, WIDTH), f32),
            vmem((8, CENTS, 128), f32),
            vmem((1, 16 * UNIT), f32),
            vmem((2, 16, 1, PART), f32),
            vmem((2, 16, 1, PART), f32),
            vmem((2, 1, PART), f32),
            vmem((2, 16, 1, PART), f32),
            vmem((2, 16, 4, 1, PART), f32),
            vmem((8, 1, CENTS), f32),
            vmem((8, 1, CENTS), f32),
            vmem((8, CENTS, WIDTH), bf16),
            vmem((8, CENTS, WIDTH), bf16),
            vmem((8, CENTS, WIDTH), bf16),
            vmem((1, CENTS, WIDTH), bf16),
            vmem((CENTS, WIDTH), f32),
            dma((3,)),
            dma((2, 8, N_PIECES)), dma((2, 8, N_PIECES)),
            dma((2, 8, N_PIECES)), dma((2, 8, N_PIECES)),
            dma((8, N_PIECES)), dma((8, N_PIECES)),
            dma((2, 16)), dma((2,)),
            dma((2, 16)), dma((2,)),
            dma((2, 16)), dma((2,)),
            dma((8,)), dma(()),
            dma((8, N_PIECES)), dma((8, N_PIECES)),
        ],
        compiler_params=pltpu.CompilerParams(
            collective_id=0, has_side_effects=True, vmem_limit_bytes=58 * 2**20
        ),
        cost_estimate=pl.CostEstimate(
            flops=4 * 4096 * 1024 * 1024, bytes_accessed=2**21, transcendentals=2**23
        ),
    )(embeddings, codebook)
    return hand_over(new, count, norm)


def solution(mesh):
    return jax.shard_map(
        local,
        mesh=mesh,
        in_specs=(P(("dp", "cent"), None), P(("cent", "dp"), None)),
        out_specs=(P(("cent", "dp"), None), P(("cent", "dp")), P(("dp", "cent"))),
        check_vma=False,
    )
```

time: 69.7 us -> 77.7 us (1.11)
  Pallas kernels: 68.8 us -> 77 us
    pallas_call x1, Pallas kernels: 67 us -> 75.1 us  [local(): pl.pallas_call(kernel, out_shape=(jax.ShapeDtypeStruct((CENTS, WIDTH), f3...]
where the time goes in v4:
time: 77.7 us; the launch traced here: 77.6 us
  Pallas kernels  77 us (99%)
    pallas_call x1, Pallas kernels, local(): pl.pallas_call(kernel, out_shape=(jax.ShapeDtypeStruct((CENTS, WIDTH), f3...  75.1 us
    pallas_call x1, Pallas kernels, hand_over(): pl.pallas_call(body, out_shape=[jax.ShapeDtypeStruct(r.shape, r.dtype) fo...  1.88 us

profile of v4, /device:TPU:1, one launch (start us, length us, event | category | flops | bytes accessed | tf_op | source)
XLA Modules:
  0.0 77.6 jit_solution(18332533618145123119)
XLA Ops:
  0.6 75.1 %shard_map.49 = (f32[128,1024]{1,0:T(8,128)}, f32[128]{0:T(128)}, f32[256]{0:T(256)}) custom-call(bf16[256,1024]{1,0:T(8,128)(2,1)} %emb.1, f32[128,1024]{1,0:T(8,128)} %book.1), custom_call_target="tpu_custom_call" | custom-call | flops 17179869184 | bytes 2097152 | tf_op jit(solution)/shard_map/pallas_call | solution.py:474
  75.7 1.9 %shard_map.50 = (f32[128,1024]{1,0:T(8,128)}, f32[128]{0:T(128)}, f32[256]{0:T(256)}) custom-call(f32[128,1024]{1,0:T(8,128)} %get-tuple-element.6.refs_0_, f32[128]{0:T(128)} %get-tuple-element.7.refs_1_, f32[256]{0:T(256)} %get-tuple-element.8.refs_2_), custom_call_target="tpu_custom_call" | custom-call | tf_op jit(solution)/shard_map/pallas_call | solution.py:463

commit v5 on v4

--- a/solution.py
+++ b/solution.py
@@ -27,6 +27,7 @@
 N_PIECES = len(PIECES)
 ORDER = (0, 1, 2, 4, 3, 5, 6, 7)
 PLACE = {mask: i for i, mask in enumerate(ORDER)}
+EARLY = 8
 NT = (((1,), (1,)), ((), ()))
 NN = (((1,), (0,)), ((), ()))
 
@@ -105,46 +106,48 @@
             return emb.at[pl.ds(r * PART + PIECES[j][0], PIECES[j][1])]
         return rows.at[row_at(r, m, 0, j)]
 
-    def row_copy(r, d, j, m):
+    def row_copy(r, w, d, j, m):
         n = m | 1 << d
         return remote(
             row_source(r, m, j), rows.at[row_at(r, n, 0, j)],
-            row_send.at[r, n, j], row_recv.at[r, n, j], row_peer(1 << d),
-        )
-
-    def cent_copy(d, j, m):
+            row_send, row_recv.at[r, w], row_peer(1 << d),
+        )
+
+    def cent_copy(w, d, j, m):
         n = m | 1 << d
         src, dst = cents.at[cent_at(m, j)], cents.at[cent_at(n, j)]
-        return remote(src, dst, cent_send.at[n, j], cent_recv.at[n, j], cent_peer(1 << d))
+        return remote(src, dst, cent_send, cent_recv.at[w], cent_peer(1 << d))
 
     def sib_copy(r, n, j):
         return remote(
             row_source(r, n, j), rows.at[row_at(r, n, 1, j)],
-            sib_send.at[r, n, j], sib_recv.at[r, n, j], row_peer(0, 1),
+            sib_send, sib_recv.at[r, PLACE[n]], row_peer(0, 1),
         )
 
     wave = waves()
+
+    def took(sem, *refs):
+        for ref in refs:
+            pltpu.make_async_copy(ref, ref, sem).wait()
 
     def row_start(r, w):
         for msg in wave[w]:
-            row_copy(r, *msg).start()
+            row_copy(r, w, *msg).start()
 
     def cent_start(w):
         for msg in wave[w]:
-            cent_copy(*msg).start()
+            cent_copy(w, *msg).start()
 
     def row_arrive(r, w):
+        took(row_recv.at[r, w], rows.at[pl.ds(0, PART)])
         for d, j, m in wave[w]:
-            row_copy(r, d, j, m).wait_recv()
             sib_copy(r, m | 1 << d, j).start()
 
     def cent_arrive(w):
-        for msg in wave[w]:
-            cent_copy(*msg).wait_recv()
+        took(cent_recv.at[w], cents.at[pl.ds(0, CENTS)])
 
     def sib_arrive(r, p):
-        for j in range(N_PIECES):
-            sib_copy(r, ORDER[p], j).wait_recv()
+        took(sib_recv.at[r, p], rows.at[pl.ds(0, PART)])
 
     def squares(half):
         @pl.loop(0, 4)
@@ -201,51 +204,47 @@
 
     def stat_copy(r, a):
         return remote(
-            lse_mine.at[r, a], lse_in.at[r, a], stat_send.at[r, a], stat_recv.at[r], slot_peer(a)
+            lse_mine.at[r, a], lse_in.at[r, a], stat_send, stat_recv.at[r], slot_peer(a)
         )
 
     def part_copy(r, a):
         return remote(
-            part_mine.at[r], part_in.at[r, a], part_send.at[r, a], part_recv.at[r], slot_peer(a)
+            part_mine.at[r], part_in.at[r, a], part_send, part_recv.at[r], slot_peer(a)
         )
 
     def fin_copy(r, a):
         return remote(
-            lse_mine.at[r, pl.ds(12, 4)], fin_in.at[r, a],
-            fin_send.at[r, a], fin_recv.at[r], slot_peer(a),
+            lse_mine.at[r, pl.ds(EARLY, 16 - EARLY)], fin_in.at[r, a],
+            fin_send, fin_recv.at[r], slot_peer(a),
         )
 
     def count_copy(n):
         return remote(
-            count_mine.at[n], count_in.at[n], count_send.at[n], count_recv, cent_peer(ORDER[n])
-        )
-
-    def wait_all(ref, sem):
-        remote(ref, ref, own_sem.at[0], sem, row_peer(0, 1)).wait_recv()
+            count_mine.at[n], count_in.at[n], count_send, count_recv, cent_peer(ORDER[n])
+        )
 
     def settled(u):
         r, p = u // 8, u % 8
-        if p < 6:
+        if 2 * p < EARLY:
             for a in (2 * p, 2 * p + 1):
                 if a:
                     stat_copy(r, a).start()
-        if p == 6:
-            wait_all(lse_in.at[r, pl.ds(1, 11)], stat_recv.at[r])
-            part_mine[r] = combine([lse_mine[r, 0]] + [lse_in[r, a] for a in range(1, 12)])
-            for a in range(1, 16):
-                part_copy(r, a).start()
         if p == 7:
             for a in range(1, 16):
                 fin_copy(r, a).start()
+            took(stat_recv.at[r], lse_in.at[r, pl.ds(1, EARLY - 1)])
+            part_mine[r] = combine([lse_mine[r, 0]] + [lse_in[r, a] for a in range(1, EARLY)])
+            for a in range(1, 16):
+                part_copy(r, a).start()
 
     def agree(r):
-        wait_all(part_in.at[r, pl.ds(1, 15)], part_recv.at[r])
-        wait_all(fin_in.at[r, pl.ds(1, 15)], fin_recv.at[r])
+        took(part_recv.at[r], part_in.at[r, pl.ds(1, 15)])
+        took(fin_recv.at[r], fin_in.at[r, pl.ds(1, 15)])
         for s in range(16):
             terms = [part_mine[r] if s == 0 else part_in[r, s]]
-            for q in range(12, 16):
+            for q in range(EARLY, 16):
                 a = mirror(s, q)
-                terms.append(lse_mine[r, q] if a == 0 else fin_in[r, a, q - 12])
+                terms.append(lse_mine[r, q] if a == 0 else fin_in[r, a, q - EARLY])
             lse = combine(terms)
             at = (r * 16 + s) * PART
             lse_all[:, at : at + PART] = lse
@@ -360,18 +359,17 @@
         at = pl.ds(*PIECES[j][:2])
         s = step_of(n, j)
         d = PIECES[j][2][s]
+        group = 3 if n in (1, 2, 4) else 0 if n == 7 else 1 + s
         box = (inbox1, inbox2, inbox3)[s]
         dst = box.at[0 if s == 2 else PLACE[n ^ 1 << d], at]
         return remote(
-            outbox.at[PLACE[n], at], dst, sum_send.at[n, j], sum_recv.at[n, j], cent_peer(1 << d)
+            outbox.at[PLACE[n], at], dst, sum_send, sum_recv.at[group], cent_peer(1 << d)
         )
 
     def gathered(n, j):
-        off, size, order = PIECES[j]
+        off, size, _ = PIECES[j]
         value = sums[PLACE[n], off : off + size, :]
         for s in range(step_of(n, j) if n else 3):
-            came = n | 1 << order[s]
-            sum_copy(came, j).wait_recv()
             box = (inbox1, inbox2, inbox3)[s]
             at = 0 if s == 2 else PLACE[n]
             value = value + box[at, off : off + size, :].astype(jnp.float32)
@@ -391,9 +389,11 @@
             send_sums(n, 0)
             count_copy(p).start()
         if p == 4:
+            took(sum_recv.at[0], inbox1.at[0])
             for m in (6, 5, 3):
                 send_sums(m, 1)
         if p == 1:
+            took(sum_recv.at[1], inbox1.at[pl.ds(0, 2)])
             for m in (4, 2, 1):
                 send_sums(m, 1)
 
@@ -422,37 +422,30 @@
         for p in range(8):
             pl.when(i == 7 - p)(functools.partial(after, p))
 
+    took(sum_recv.at[2], inbox2.at[0])
     for n in (4, 2, 1):
         send_sums(n, 2)
 
-    for w in range(7):
-        for msg in wave[w]:
-            row_copy(0, *msg).wait_send()
-            row_copy(1, *msg).wait_send()
-            cent_copy(*msg).wait_send()
+    took(row_send, rows.at[pl.ds(0, 14 * PART)])
+    took(sib_send, rows.at[pl.ds(0, 16 * PART)])
+    took(cent_send, cents.at[pl.ds(0, 7 * CENTS)])
     for r in range(2):
-        for n in range(8):
-            for j in range(N_PIECES):
-                sib_copy(r, n, j).wait_send()
-        for a in range(1, 16):
-            if a < 12:
-                stat_copy(r, a).wait_send()
-            part_copy(r, a).wait_send()
-            fin_copy(r, a).wait_send()
-    wait_all(count_in.at[pl.ds(1, 7)], count_recv)
+        took(stat_send, lse_in.at[r, pl.ds(1, EARLY - 1)])
+        took(part_send, part_in.at[r, pl.ds(1, 15)])
+        took(fin_send, fin_in.at[r, pl.ds(1, 15)])
+    took(count_send, count_in.at[pl.ds(1, 7)])
+    took(count_recv, count_in.at[pl.ds(1, 7)])
     count = functools.reduce(jnp.add, [count_mine[0]] + [count_in[n] for n in range(1, 8)])
     count_out[...] = count.reshape(CENTS)
     below = jnp.broadcast_to(count, (CENTS, 128)).T + PRIOR
+    took(sum_recv.at[3], inbox1.at[pl.ds(0, 3)])
     for j in range(N_PIECES):
         off, size, _ = PIECES[j]
         top = gathered(0, j) + PRIOR * book_in[off : off + size, :]
         for q in range(WIDTH // 128):
             cols = slice(q * 128, (q + 1) * 128)
             new_out[off : off + size, cols] = top[:, cols] / below[off : off + size, :]
-    for n in range(1, 8):
-        count_copy(n).wait_send()
-        for j in range(N_PIECES):
-            sum_copy(n, j).wait_send()
+    took(sum_send, outbox.at[pl.ds(1, 7)])
 
 
 def hand_over(*results):
@@ -493,7 +486,7 @@
             vmem((2, 16, 1, PART), f32),
             vmem((2, 1, PART), f32),
             vmem((2, 16, 1, PART), f32),
-            vmem((2, 16, 4, 1, PART), f32),
+            vmem((2, 16, 16 - EARLY, 1, PART), f32),
             vmem((8, 1, CENTS), f32),
             vmem((8, 1, CENTS), f32),
             vmem((8, CENTS, WIDTH), bf16),
@@ -502,14 +495,14 @@
             vmem((1, CENTS, WIDTH), bf16),
             vmem((CENTS, WIDTH), f32),
             dma((3,)),
-            dma((2, 8, N_PIECES)), dma((2, 8, N_PIECES)),
-            dma((2, 8, N_PIECES)), dma((2, 8, N_PIECES)),
-            dma((8, N_PIECES)), dma((8, N_PIECES)),
-            dma((2, 16)), dma((2,)),
-            dma((2, 16)), dma((2,)),
-            dma((2, 16)), dma((2,)),
-            dma((8,)), dma(()),
-            dma((8, N_PIECES)), dma((8, N_PIECES)),
+            dma(()), dma((2, 7)),
+            dma(()), dma((2, 8)),
+            dma(()), dma((7,)),
+            dma(()), dma((2,)),
+            dma(()), dma((2,)),
+            dma(()), dma((2,)),
+            dma(()), dma(()),
+            dma(()), dma((4,)),
         ],
         compiler_params=pltpu.CompilerParams(
             collective_id=0, has_side_effects=True, vmem_limit_bytes=58 * 2**20

time: 77.7 us -> 68.1 us (0.88)
  Pallas kernels: 77 us -> 67.3 us
    pallas_call x1, Pallas kernels: 75.1 us -> 65.4 us  [local(): pl.pallas_call(kernel, out_shape=(jax.ShapeDtypeStruct((CENTS, WIDTH), f3...]
where the time goes in v5:
time: 68.1 us; the launch traced here: 68 us
  Pallas kernels  67.3 us (99%)
    pallas_call x1, Pallas kernels, local(): pl.pallas_call(kernel, out_shape=(jax.ShapeDtypeStruct((CENTS, WIDTH), f3...  65.4 us
    pallas_call x1, Pallas kernels, hand_over(): pl.pallas_call(body, out_shape=[jax.ShapeDtypeStruct(r.shape, r.dtype) fo...  1.88 us

profile of v5, /device:TPU:1, one launch (start us, length us, event | category | flops | bytes accessed | tf_op | source)
XLA Modules:
  0.0 68.0 jit_solution(18019978449119857209)
XLA Ops:
  0.6 65.4 %shard_map.49 = (f32[128,1024]{1,0:T(8,128)}, f32[128]{0:T(128)}, f32[256]{0:T(256)}) custom-call(bf16[256,1024]{1,0:T(8,128)(2,1)} %emb.1, f32[128,1024]{1,0:T(8,128)} %book.1), custom_call_target="tpu_custom_call" | custom-call | flops 17179869184 | bytes 2097152 | tf_op jit(solution)/shard_map/pallas_call | solution.py:467
  66.1 1.9 %shard_map.50 = (f32[128,1024]{1,0:T(8,128)}, f32[128]{0:T(128)}, f32[256]{0:T(256)}) custom-call(f32[128,1024]{1,0:T(8,128)} %get-tuple-element.6.refs_0_, f32[128]{0:T(128)} %get-tuple-element.7.refs_1_, f32[256]{0:T(256)} %get-tuple-element.8.refs_2_), custom_call_target="tpu_custom_call" | custom-call | tf_op jit(solution)/shard_map/pallas_call | solution.py:456

commit v6 on v5

--- a/solution.py
+++ b/solution.py
@@ -41,6 +41,24 @@
     return wave
 
 
+def wave_of(j, mask):
+    a, b, c = (1 << d for d in PIECES[j][2])
+    return (a, b, c, a | b, a | c, b | c, 7).index(mask)
+
+
+def mask_of(j, w):
+    return next(mask for mask in range(1, 8) if wave_of(j, mask) == w)
+
+
+def mosaic(rows):
+    lane = lax.broadcasted_iota(jnp.int32, (1, PART), 1)
+    whole = rows[-1]
+    for (off, _, _), (end, _, _), row in list(zip(PIECES, PIECES[1:], rows))[::-1]:
+        if row is not whole:
+            whole = jnp.where((lane >= off) & (lane < end), row, whole)
+    return whole
+
+
 def combine(terms):
     top = functools.reduce(jnp.maximum, terms)
     total = functools.reduce(jnp.add, [jnp.exp2(t - top) for t in terms])
@@ -50,7 +68,7 @@
 def kernel(
     emb, book, new_out, count_out, norm_out,
     rows, cents, scores, half_sq, peak, sums, tally, lse_all,
-    lse_mine, lse_in, part_mine, part_in, fin_in, count_mine, count_in,
+    lse_unit, lse_mine, lse_in, part_mine, part_in, fin_in, count_mine, count_in,
     outbox, inbox1, inbox2, inbox3,
     book_in, own_sem, row_send, row_recv, sib_send, sib_recv, cent_send, cent_recv,
     stat_send, stat_recv, part_send, part_recv, fin_send, fin_recv,
@@ -95,34 +113,28 @@
     own[1].start()
     pl.semaphore_wait(barrier, len(peers))
 
-    def row_at(r, n, k, j):
-        return pl.ds((r * 8 + PLACE[n]) * UNIT + k * PART + PIECES[j][0], PIECES[j][1])
+    def row_at(r, n, j):
+        return pl.ds((r * 8 + 1 + wave_of(j, n)) * UNIT + PIECES[j][0], PIECES[j][1])
 
     def cent_at(n, j):
         return pl.ds(PLACE[n] * CENTS + PIECES[j][0], PIECES[j][1])
 
-    def row_source(r, m, j):
-        if m == 0:
-            return emb.at[pl.ds(r * PART + PIECES[j][0], PIECES[j][1])]
-        return rows.at[row_at(r, m, 0, j)]
-
     def row_copy(r, w, d, j, m):
-        n = m | 1 << d
-        return remote(
-            row_source(r, m, j), rows.at[row_at(r, n, 0, j)],
-            row_send, row_recv.at[r, w], row_peer(1 << d),
-        )
+        off, size, _ = PIECES[j]
+        src = rows.at[row_at(r, m, j)] if m else emb.at[pl.ds(r * PART + off, size)]
+        dst = rows.at[row_at(r, m | 1 << d, j)]
+        return remote(src, dst, row_send, row_recv.at[r, w], row_peer(1 << d))
 
     def cent_copy(w, d, j, m):
         n = m | 1 << d
         src, dst = cents.at[cent_at(m, j)], cents.at[cent_at(n, j)]
         return remote(src, dst, cent_send, cent_recv.at[w], cent_peer(1 << d))
 
-    def sib_copy(r, n, j):
-        return remote(
-            row_source(r, n, j), rows.at[row_at(r, n, 1, j)],
-            sib_send, sib_recv.at[r, PLACE[n]], row_peer(0, 1),
-        )
+    def sib_copy(r, i):
+        at = (r * 8 + i) * UNIT
+        src = rows.at[pl.ds(at, PART)] if i else emb.at[pl.ds(r * PART, PART)]
+        dst = rows.at[pl.ds(at + PART, PART)]
+        return remote(src, dst, sib_send, sib_recv.at[r, i], row_peer(0, 1))
 
     wave = waves()
 
@@ -140,14 +152,13 @@
 
     def row_arrive(r, w):
         took(row_recv.at[r, w], rows.at[pl.ds(0, PART)])
-        for d, j, m in wave[w]:
-            sib_copy(r, m | 1 << d, j).start()
+        sib_copy(r, 1 + w).start()
 
     def cent_arrive(w):
         took(cent_recv.at[w], cents.at[pl.ds(0, CENTS)])
 
-    def sib_arrive(r, p):
-        took(sib_recv.at[r, p], rows.at[pl.ds(0, PART)])
+    def sib_arrive(u):
+        took(sib_recv.at[u // 8, u % 8], rows.at[pl.ds(0, PART)])
 
     def squares(half):
         @pl.loop(0, 4)
@@ -187,9 +198,8 @@
 
     def settle(u, high, total):
         lse = high + jnp.log2(jnp.sum(total, axis=0, keepdims=True))
-        r, p = u // 8, u % 8
-        lse_mine[r, 2 * p] = lse[:, :PART]
-        lse_mine[r, 2 * p + 1] = lse[:, PART:]
+        lse_unit[u, 0] = lse[:, :PART]
+        lse_unit[u, 1] = lse[:, PART:]
 
     def soften(u):
         high = jnp.max(peak[u], axis=0, keepdims=True)
@@ -224,12 +234,17 @@
         )
 
     def settled(u):
-        r, p = u // 8, u % 8
-        if 2 * p < EARLY:
-            for a in (2 * p, 2 * p + 1):
-                if a:
-                    stat_copy(r, a).start()
-        if p == 7:
+        r, i = u // 8, u % 8
+        if i in (3, 7):
+            for a in range(0, EARLY) if i == 3 else range(EARLY, 16):
+                n, k = ORDER[a // 2], a % 2
+                units = [r * 8 + (1 + wave_of(j, n) if n else 0) for j in range(N_PIECES)]
+                known = {v: lse_unit[v, k] for v in set(units)}
+                lse_mine[r, a] = mosaic([known[v] for v in units])
+        if i == 3:
+            for a in range(1, EARLY):
+                stat_copy(r, a).start()
+        if i == 7:
             for a in range(1, 16):
                 fin_copy(r, a).start()
             took(stat_recv.at[r], lse_in.at[r, pl.ds(1, EARLY - 1)])
@@ -240,97 +255,19 @@
     def agree(r):
         took(part_recv.at[r], part_in.at[r, pl.ds(1, 15)])
         took(fin_recv.at[r], fin_in.at[r, pl.ds(1, 15)])
+        agreed = []
         for s in range(16):
             terms = [part_mine[r] if s == 0 else part_in[r, s]]
             for q in range(EARLY, 16):
                 a = mirror(s, q)
                 terms.append(lse_mine[r, q] if a == 0 else fin_in[r, a, q - EARLY])
-            lse = combine(terms)
-            at = (r * 16 + s) * PART
-            lse_all[:, at : at + PART] = lse
-            if s == 0:
-                norm_out[r * PART : (r + 1) * PART] = (lse * LN2).reshape(PART)
-
-    for w in range(3):
-        row_start(0, w)
-    own[2].wait()
-    cents[0:CENTS, :] = book_in[...].astype(jnp.bfloat16)
-    for w in range(3):
-        cent_start(w)
-    for r in range(2):
-        for j in range(N_PIECES):
-            sib_copy(r, 0, j).start()
-    own[0].wait()
-    own[1].wait()
-    cent_arrive(0)
-    cent_start(3)
-    cent_start(4)
-    row_arrive(0, 0)
-    row_start(0, 3)
-    row_start(0, 4)
-    cent_arrive(1)
-    cent_start(5)
-    row_arrive(0, 1)
-    row_start(0, 5)
-    cent_arrive(2)
-    squares(0)
-    row_arrive(0, 2)
-    cent_arrive(3)
-    cent_start(6)
-    row_arrive(0, 3)
-    row_start(0, 6)
-    row_start(1, 0)
-    for p in range(4):
-        sib_arrive(0, p)
-
-    @pl.loop(0, 4)
-    def _(u):
-        score(u, (0, 1), True)
-
-    row_arrive(0, 4)
-    cent_arrive(4)
-    row_arrive(0, 5)
-    row_start(1, 1)
-    row_start(1, 2)
-    cent_arrive(5)
-    row_arrive(0, 6)
-    cent_arrive(6)
-    squares(1)
-    score(0, (2, 3), False)
-
-    @pl.loop(1, 4)
-    def _(u):
-        @pl.when(u == 2)
-        def _():
-            row_arrive(1, 0)
-            row_start(1, 3)
-            row_start(1, 4)
-
-        score(u, (2, 3), False, u - 1)
-        for v in range(3):
-            pl.when(u == v + 1)(functools.partial(settled, v))
-
-    def before(u):
-        if u == 5:
-            row_arrive(1, 1)
-            row_start(1, 5)
-        if u == 8:
-            row_arrive(1, 2)
-        if u == 10:
-            row_arrive(1, 3)
-            row_start(1, 6)
-        if u == 14:
-            row_arrive(1, 6)
-        sib_arrive(u // 8, u % 8)
-
-    def unit_loop(lo, hi):
-        @pl.loop(lo, hi)
-        def _(u):
-            for v in range(lo, hi):
-                pl.when(u == v)(functools.partial(before, v))
-            score(u, (0, 1, 2, 3), True, u - 1)
-            for v in range(lo, hi):
-                pl.when(u == v)(functools.partial(settled, v - 1))
+            agreed.append(combine(terms))
+        norm_out[r * PART : (r + 1) * PART] = (agreed[0] * LN2).reshape(PART)
+        for i in range(8):
+            masks = [mask_of(j, i - 1) if i else 0 for j in range(N_PIECES)]
+            for k in range(2):
+                at = (r * 8 + i) * UNIT + k * PART
+                lse_all[:, at : at + PART] = mosaic([agreed[2 * PLACE[n] + k] for n in masks])
 
     def weigh(p, r):
         at = pl.ds(pl.multiple_of(p * CENTS, CENTS), CENTS)
@@ -352,6 +289,102 @@
         else:
             tally[p] = count
 
+    for w in range(3):
+        row_start(0, w)
+    own[2].wait()
+    cents[0:CENTS, :] = book_in[...].astype(jnp.bfloat16)
+    for w in range(3):
+        cent_start(w)
+    sib_copy(0, 0).start()
+    sib_copy(1, 0).start()
+    own[0].wait()
+    own[1].wait()
+    cent_arrive(0)
+    cent_start(3)
+    cent_start(4)
+    row_arrive(0, 0)
+    row_start(0, 3)
+    row_start(0, 4)
+    cent_arrive(1)
+    cent_start(5)
+    row_arrive(0, 1)
+    row_start(0, 5)
+    cent_arrive(2)
+    squares(0)
+    row_arrive(0, 2)
+
+    first = (0, 8, 1, 2, 3, 4, 5, 6)
+
+    def first_unit(i):
+        return jnp.where(i == 0, 0, jnp.where(i == 1, 8, i - 1))
+
+    def before_first(i):
+        if i == 5:
+            cent_arrive(3)
+            cent_start(6)
+            row_arrive(0, 3)
+            row_start(0, 6)
+            row_start(1, 0)
+        if i == 6:
+            row_arrive(0, 4)
+            cent_arrive(4)
+        if i == 7:
+            row_arrive(0, 5)
+            row_start(1, 1)
+            row_start(1, 2)
+            cent_arrive(5)
+        sib_arrive(first[i])
+
+    @pl.loop(0, 8)
+    def _(i):
+        for v in range(8):
+            pl.when(i == v)(functools.partial(before_first, v))
+        score(first_unit(i), (0, 1), True)
+
+    row_arrive(0, 6)
+    cent_arrive(6)
+    squares(1)
+    score(0, (2, 3), False)
+
+    @pl.loop(1, 8)
+    def _(i):
+        @pl.when(i == 3)
+        def _():
+            row_arrive(1, 0)
+            row_start(1, 3)
+            row_start(1, 4)
+
+        score(first_unit(i), (2, 3), False, first_unit(i - 1))
+        pl.when(i == 5)(functools.partial(settled, 3))
+
+    def before_full(i):
+        if i == 2:
+            row_arrive(1, 1)
+            row_start(1, 5)
+        if i == 3:
+            row_arrive(1, 2)
+        if i == 4:
+            row_arrive(1, 3)
+            row_start(1, 6)
+            agree(0)
+        if i > 4:
+            row_arrive(1, i - 1)
+
+    @pl.loop(0, 8)
+    def _(i):
+        for v in range(2, 8):
+            pl.when(i == v)(functools.partial(before_full, v))
+        pl.when(i > 4)(lambda: weigh(12 - i, 0))
+        for v in range(8):
+            pl.when(i == v)(functools.partial(sib_arrive, v + 8 if v else 7))
+        last = jnp.where(i == 0, 6, jnp.where(i == 1, 7, 7 + i))
+        score(jnp.where(i == 0, 7, 8 + i), (0, 1, 2, 3), True, last)
+        pl.when(i == 1)(functools.partial(settled, 7))
+        pl.when(i == 4)(functools.partial(settled, 11))
+
+    soften(15)
+    settled(15)
+
     def step_of(n, j):
         return next(s for s in range(3) if n >> PIECES[j][2][s] & 1)
 
@@ -396,19 +429,6 @@
             took(sum_recv.at[1], inbox1.at[pl.ds(0, 2)])
             for m in (4, 2, 1):
                 send_sums(m, 1)
-
-    unit_loop(4, 12)
-    agree(0)
-
-    @pl.loop(0, 3)
-    def _(i):
-        weigh(7 - i, 0)
-        pl.when(i == 0)(functools.partial(row_arrive, 1, 4))
-
-    row_arrive(1, 5)
-    unit_loop(12, 16)
-    soften(15)
-    settled(15)
 
     @pl.loop(3, 8)
     def _(i):
@@ -482,6 +502,7 @@
             vmem((8, CENTS, WIDTH), f32),
             vmem((8, CENTS, 128), f32),
             vmem((1, 16 * UNIT), f32),
+            vmem((16, 2, 1, PART), f32),
             vmem((2, 16, 1, PART), f32),
             vmem((2, 16, 1, PART), f32),
             vmem((2, 1, PART), f32),

time: 68.1 us -> 71.8 us (1.054)
  Pallas kernels: 67.3 us -> 71.1 us
    pallas_call x1, Pallas kernels: 65.4 us -> 69.2 us  [local(): pl.pallas_call(kernel, out_shape=(jax.ShapeDtypeStruct((CENTS, WIDTH), f3...]
where the time goes in v6:
time: 71.8 us; the launch traced here: 71.7 us
  Pallas kernels  71.1 us (99%)
    pallas_call x1, Pallas kernels, local(): pl.pallas_call(kernel, out_shape=(jax.ShapeDtypeStruct((CENTS, WIDTH), f3...  69.2 us
    pallas_call x1, Pallas kernels, hand_over(): pl.pallas_call(body, out_shape=[jax.ShapeDtypeStruct(r.shape, r.dtype) fo...  1.88 us

profile of v6, /device:TPU:1, one launch (start us, length us, event | category | flops | bytes accessed | tf_op | source)
XLA Modules:
  0.0 71.7 jit_solution(8132060354466453078)
XLA Ops:
  0.6 69.2 %shard_map.49 = (f32[128,1024]{1,0:T(8,128)}, f32[128]{0:T(128)}, f32[256]{0:T(256)}) custom-call(bf16[256,1024]{1,0:T(8,128)(2,1)} %emb.1, f32[128,1024]{1,0:T(8,128)} %book.1), custom_call_target="tpu_custom_call" | custom-call | flops 17179869184 | bytes 2097152 | tf_op jit(solution)/shard_map/pallas_call | solution.py:487
  69.8 1.9 %shard_map.50 = (f32[128,1024]{1,0:T(8,128)}, f32[128]{0:T(128)}, f32[256]{0:T(256)}) custom-call(f32[128,1024]{1,0:T(8,128)} %get-tuple-element.6.refs_0_, f32[128]{0:T(128)} %get-tuple-element.7.refs_1_, f32[256]{0:T(256)} %get-tuple-element.8.refs_2_), custom_call_target="tpu_custom_call" | custom-call | tf_op jit(solution)/shard_map/pallas_call | solution.py:476

commit v7 on v6

--- a/solution.py
+++ b/solution.py
@@ -319,20 +319,22 @@
         return jnp.where(i == 0, 0, jnp.where(i == 1, 8, i - 1))
 
     def before_first(i):
-        if i == 5:
+        if i == 4:
             cent_arrive(3)
             cent_start(6)
             row_arrive(0, 3)
             row_start(0, 6)
             row_start(1, 0)
-        if i == 6:
+        if i == 5:
             row_arrive(0, 4)
             cent_arrive(4)
-        if i == 7:
+        if i == 6:
             row_arrive(0, 5)
             row_start(1, 1)
             row_start(1, 2)
             cent_arrive(5)
+        if i == 7:
+            row_arrive(0, 6)
         sib_arrive(first[i])
 
     @pl.loop(0, 8)
@@ -341,7 +343,6 @@
             pl.when(i == v)(functools.partial(before_first, v))
         score(first_unit(i), (0, 1), True)
 
-    row_arrive(0, 6)
     cent_arrive(6)
     squares(1)
     score(0, (2, 3), False)
@@ -358,25 +359,26 @@
         pl.when(i == 5)(functools.partial(settled, 3))
 
     def before_full(i):
-        if i == 2:
+        if i == 1:
             row_arrive(1, 1)
             row_start(1, 5)
+        if i == 2:
+            row_arrive(1, 2)
         if i == 3:
-            row_arrive(1, 2)
-        if i == 4:
             row_arrive(1, 3)
             row_start(1, 6)
+        if i == 5:
             agree(0)
-        if i > 4:
-            row_arrive(1, i - 1)
+        if i in (5, 6):
+            weigh(12 - i, 0)
+        if i in (4, 5, 6):
+            row_arrive(1, i)
+        sib_arrive(i + 8 if i else 7)
 
     @pl.loop(0, 8)
     def _(i):
-        for v in range(2, 8):
+        for v in range(8):
             pl.when(i == v)(functools.partial(before_full, v))
-        pl.when(i > 4)(lambda: weigh(12 - i, 0))
-        for v in range(8):
-            pl.when(i == v)(functools.partial(sib_arrive, v + 8 if v else 7))
         last = jnp.where(i == 0, 6, jnp.where(i == 1, 7, 7 + i))
         score(jnp.where(i == 0, 7, 8 + i), (0, 1, 2, 3), True, last)
         pl.when(i == 1)(functools.partial(settled, 7))
@@ -430,7 +432,7 @@
             for m in (4, 2, 1):
                 send_sums(m, 1)
 
-    @pl.loop(3, 8)
+    @pl.loop(2, 8)
     def _(i):
         weigh(7 - i, 0)
 

time: 71.8 us -> 66.1 us (0.921)
  Pallas kernels: 71.1 us -> 65.3 us
    pallas_call x1, Pallas kernels: 69.2 us -> 63.4 us  [local(): pl.pallas_call(kernel, out_shape=(jax.ShapeDtypeStruct((CENTS, WIDTH), f3...]
where the time goes in v7:
time: 66.1 us; the launch traced here: 66 us
  Pallas kernels  65.3 us (99%)
    pallas_call x1, Pallas kernels, local(): pl.pallas_call(kernel, out_shape=(jax.ShapeDtypeStruct((CENTS, WIDTH), f3...  63.4 us
    pallas_call x1, Pallas kernels, hand_over(): pl.pallas_call(body, out_shape=[jax.ShapeDtypeStruct(r.shape, r.dtype) fo...  1.88 us

profile of v7, /device:TPU:1, one launch (start us, length us, event | category | flops | bytes accessed | tf_op | source)
XLA Modules:
  0.0 66.0 jit_solution(5552788534310805938)
XLA Ops:
  0.6 63.4 %shard_map.49 = (f32[128,1024]{1,0:T(8,128)}, f32[128]{0:T(128)}, f32[256]{0:T(256)}) custom-call(bf16[256,1024]{1,0:T(8,128)(2,1)} %emb.1, f32[128,1024]{1,0:T(8,128)} %book.1), custom_call_target="tpu_custom_call" | custom-call | flops 17179869184 | bytes 2097152 | tf_op jit(solution)/shard_map/pallas_call | solution.py:489
  64.1 1.9 %shard_map.50 = (f32[128,1024]{1,0:T(8,128)}, f32[128]{0:T(128)}, f32[256]{0:T(256)}) custom-call(f32[128,1024]{1,0:T(8,128)} %get-tuple-element.6.refs_0_, f32[128]{0:T(128)} %get-tuple-element.7.refs_1_, f32[256]{0:T(256)} %get-tuple-element.8.refs_2_), custom_call_target="tpu_custom_call" | custom-call | tf_op jit(solution)/shard_map/pallas_call | solution.py:478

commit v8 on v7

--- a/solution.py
+++ b/solution.py
@@ -470,28 +470,15 @@
     took(sum_send, outbox.at[pl.ds(1, 7)])
 
 
-def hand_over(*results):
-    def body(*refs):
-        for i in range(3):
-            refs[3 + i][...] = refs[i][...]
-
-    return pl.pallas_call(
-        body,
-        out_shape=[jax.ShapeDtypeStruct(r.shape, r.dtype) for r in results],
-        in_specs=[pl.BlockSpec(memory_space=pltpu.VMEM)] * 3,
-        out_specs=[pl.BlockSpec(memory_space=pltpu.VMEM)] * 3,
-    )(*results)
-
-
 def local(embeddings, codebook):
     f32, bf16 = jnp.float32, jnp.bfloat16
     vmem, dma = pltpu.VMEM, pltpu.SemaphoreType.DMA
     new, count, norm = pl.pallas_call(
         kernel,
         out_shape=(
-            jax.ShapeDtypeStruct((CENTS, WIDTH), f32),
-            jax.ShapeDtypeStruct((CENTS,), f32),
-            jax.ShapeDtypeStruct((ROWS,), f32),
+            vmem((CENTS, WIDTH), f32),
+            vmem((CENTS,), f32),
+            vmem((ROWS,), f32),
         ),
         in_specs=[pl.BlockSpec(memory_space=pl.ANY)] * 2,
         out_specs=[pl.BlockSpec(memory_space=pltpu.VMEM)] * 3,
@@ -534,7 +521,7 @@
             flops=4 * 4096 * 1024 * 1024, bytes_accessed=2**21, transcendentals=2**23
         ),
     )(embeddings, codebook)
-    return hand_over(new, count, norm)
+    return new, count, norm
 
 
 def solution(mesh):

time: 66.1 us -> 65.2 us (0.986)
  Pallas kernels: 65.3 us -> 62.6 us
  local copies, waits for them, and re-layouts: 0 us -> 1.87 us
    pallas_call x2 -> x1, Pallas kernels: 65.3 us -> 62.6 us  [local(): pl.pallas_call(kernel, out_shape=(vmem((CENTS, WIDTH), f32), vmem((CENTS,...]
    unnamed x0 -> x3, local copies, waits for them, and re-layouts: none -> 1.87 us
where the time goes in v8:
time: 65.2 us; the launch traced here: 65.1 us
  Pallas kernels  62.6 us (96%)
  local copies, waits for them, and re-layouts  1.87 us (3%)
    pallas_call x1, Pallas kernels, local(): pl.pallas_call(kernel, out_shape=(vmem((CENTS, WIDTH), f32), vmem((CENTS,...  62.6 us
    unnamed x3, local copies, waits for them, and re-layouts  1.87 us

profile of v8, /device:TPU:1, one launch (start us, length us, event | category | flops | bytes accessed | tf_op | source)
XLA Modules:
  0.0 65.1 jit_solution(4956025532511247259)
XLA Ops:
  0.6 62.6 %shard_map.49 = (f32[128,1024]{1,0:T(8,128)S(1)}, f32[128]{0:T(128)S(1)}, f32[256]{0:T(256)S(1)}) custom-call(bf16[256,1024]{1,0:T(8,128)(2,1)} %emb.1, f32[128,1024]{1,0:T(8,128)} %book.1), custom_call_target="tpu_custom_call" | custom-call | flops 17179869184 | bytes 2097152 | tf_op jit(solution)/shard_map/pallas_call | solution.py:476
  63.2 0.8 %copy.8 = f32[128,1024]{1,0:T(8,128)} copy(f32[128,1024]{1,0:T(8,128)S(1)} %get-tuple-element.3) | data formatting | bytes 1048576
  64.0 0.5 copy.9
  64.6 0.6 copy.10

commit v9 on v8

--- a/solution.py
+++ b/solution.py
@@ -394,7 +394,7 @@
         at = pl.ds(*PIECES[j][:2])
         s = step_of(n, j)
         d = PIECES[j][2][s]
-        group = 3 if n in (1, 2, 4) else 0 if n == 7 else 1 + s
+        group = 0 if n == 7 else 1 + s if n in (3, 5, 6) else 3 + s // 2
         box = (inbox1, inbox2, inbox3)[s]
         dst = box.at[0 if s == 2 else PLACE[n ^ 1 << d], at]
         return remote(
@@ -402,12 +402,10 @@
         )
 
     def gathered(n, j):
-        off, size, _ = PIECES[j]
-        value = sums[PLACE[n], off : off + size, :]
-        for s in range(step_of(n, j) if n else 3):
-            box = (inbox1, inbox2, inbox3)[s]
-            at = 0 if s == 2 else PLACE[n]
-            value = value + box[at, off : off + size, :].astype(jnp.float32)
+        at = PLACE[n], slice(PIECES[j][0], PIECES[j][0] + PIECES[j][1])
+        value = sums[at]
+        for box in (inbox1, inbox2)[: step_of(n, j)]:
+            value = value + box[at].astype(jnp.float32)
         return value
 
     def send_sums(n, step):
@@ -432,7 +430,7 @@
             for m in (4, 2, 1):
                 send_sums(m, 1)
 
-    @pl.loop(2, 8)
+    @pl.loop(2, 6)
     def _(i):
         weigh(7 - i, 0)
 
@@ -440,6 +438,7 @@
 
     @pl.loop(0, 8)
     def _(i):
+        pl.when(i > 5)(lambda: weigh(7 - i, 0))
         weigh(7 - i, 1)
         for p in range(8):
             pl.when(i == 7 - p)(functools.partial(after, p))
@@ -460,13 +459,18 @@
     count = functools.reduce(jnp.add, [count_mine[0]] + [count_in[n] for n in range(1, 8)])
     count_out[...] = count.reshape(CENTS)
     below = jnp.broadcast_to(count, (CENTS, 128)).T + PRIOR
-    took(sum_recv.at[3], inbox1.at[pl.ds(0, 3)])
-    for j in range(N_PIECES):
-        off, size, _ = PIECES[j]
-        top = gathered(0, j) + PRIOR * book_in[off : off + size, :]
-        for q in range(WIDTH // 128):
-            cols = slice(q * 128, (q + 1) * 128)
-            new_out[off : off + size, cols] = top[:, cols] / below[off : off + size, :]
+    took(sum_recv.at[3], inbox1.at[pl.ds(0, 2)])
+    share = 1.0 / below
+    for q in range(WIDTH // 128):
+        cols = slice(q * 128, (q + 1) * 128)
+        near = sums[0, :, cols] + PRIOR * book_in[:, cols]
+        for box in (inbox1, inbox2):
+            near = near + box[0, :, cols].astype(jnp.float32)
+        sums[0, :, cols] = near
+    took(sum_recv.at[4], inbox3.at[0])
+    for q in range(WIDTH // 128):
+        cols = slice(q * 128, (q + 1) * 128)
+        new_out[:, cols] = (sums[0, :, cols] + inbox3[0, :, cols].astype(jnp.float32)) * share
     took(sum_send, outbox.at[pl.ds(1, 7)])
 
 
@@ -512,7 +516,7 @@
             dma(()), dma((2,)),
             dma(()), dma((2,)),
             dma(()), dma(()),
-            dma(()), dma((4,)),
+            dma(()), dma((5,)),
         ],
         compiler_params=pltpu.CompilerParams(
             collective_id=0, has_side_effects=True, vmem_limit_bytes=58 * 2**20

time: 65.2 us -> 64.2 us (0.985)
  Pallas kernels: 62.6 us -> 61.6 us
    pallas_call x1, Pallas kernels: 62.6 us -> 61.6 us  [local(): pl.pallas_call(kernel, out_shape=(vmem((CENTS, WIDTH), f32), vmem((CENTS,...]
where the time goes in v9:
time: 64.2 us; the launch traced here: 64.1 us
  Pallas kernels  61.6 us (96%)
  local copies, waits for them, and re-layouts  1.87 us (3%)
    pallas_call x1, Pallas kernels, local(): pl.pallas_call(kernel, out_shape=(vmem((CENTS, WIDTH), f32), vmem((CENTS,...  61.6 us
    unnamed x3, local copies, waits for them, and re-layouts  1.87 us

profile of v9, /device:TPU:1, one launch (start us, length us, event | category | flops | bytes accessed | tf_op | source)
XLA Modules:
  0.0 64.1 jit_solution(14134974539433740064)
XLA Ops:
  0.6 61.6 %shard_map.49 = (f32[128,1024]{1,0:T(8,128)S(1)}, f32[128]{0:T(128)S(1)}, f32[256]{0:T(256)S(1)}) custom-call(bf16[256,1024]{1,0:T(8,128)(2,1)} %emb.1, f32[128,1024]{1,0:T(8,128)} %book.1), custom_call_target="tpu_custom_call" | custom-call | flops 17179869184 | bytes 2097152 | tf_op jit(solution)/shard_map/pallas_call | solution.py:480
  62.3 0.8 %copy.8 = f32[128,1024]{1,0:T(8,128)} copy(f32[128,1024]{1,0:T(8,128)S(1)} %get-tuple-element.3) | data formatting | bytes 1048576
  63.1 0.5 copy.9
  63.6 0.6 copy.10

commit v10 on v9

--- a/solution.py
+++ b/solution.py
@@ -367,10 +367,9 @@
         if i == 3:
             row_arrive(1, 3)
             row_start(1, 6)
-        if i == 5:
+        if i == 6:
             agree(0)
-        if i in (5, 6):
-            weigh(12 - i, 0)
+            weigh(7, 0)
         if i in (4, 5, 6):
             row_arrive(1, i)
         sib_arrive(i + 8 if i else 7)
@@ -430,7 +429,7 @@
             for m in (4, 2, 1):
                 send_sums(m, 1)
 
-    @pl.loop(2, 6)
+    @pl.loop(1, 5)
     def _(i):
         weigh(7 - i, 0)
 
@@ -438,7 +437,7 @@
 
     @pl.loop(0, 8)
     def _(i):
-        pl.when(i > 5)(lambda: weigh(7 - i, 0))
+        pl.when(i > 4)(lambda: weigh(7 - i, 0))
         weigh(7 - i, 1)
         for p in range(8):
             pl.when(i == 7 - p)(functools.partial(after, p))

time: 64.2 us -> 63.8 us (level); the launches traced: 64.1 us -> 63 us
  Pallas kernels: 61.6 us -> 60.5 us
    pallas_call x1, Pallas kernels: 61.6 us -> 60.5 us  [local(): pl.pallas_call(kernel, out_shape=(vmem((CENTS, WIDTH), f32), vmem((CENTS,...]
where the time goes in v10:
time: 63.8 us; the launch traced here: 63 us
  Pallas kernels  60.5 us (95%)
  local copies, waits for them, and re-layouts  1.87 us (3%)
  between operations  0.64 us (1%)
    pallas_call x1, Pallas kernels, local(): pl.pallas_call(kernel, out_shape=(vmem((CENTS, WIDTH), f32), vmem((CENTS,...  60.5 us
    unnamed x3, local copies, waits for them, and re-layouts  1.87 us

profile of v10, /device:TPU:1, one launch (start us, length us, event | category | flops | bytes accessed | tf_op | source)
XLA Modules:
  0.0 63.0 jit_solution(12972639050575473469)
XLA Ops:
  0.6 60.5 %shard_map.49 = (f32[128,1024]{1,0:T(8,128)S(1)}, f32[128]{0:T(128)S(1)}, f32[256]{0:T(256)S(1)}) custom-call(bf16[256,1024]{1,0:T(8,128)(2,1)} %emb.1, f32[128,1024]{1,0:T(8,128)} %book.1), custom_call_target="tpu_custom_call" | custom-call | flops 17179869184 | bytes 2097152 | tf_op jit(solution)/shard_map/pallas_call | solution.py:479
  61.1 0.8 %copy.8 = f32[128,1024]{1,0:T(8,128)} copy(f32[128,1024]{1,0:T(8,128)S(1)} %get-tuple-element.3) | data formatting | bytes 1048576
  61.9 0.5 copy.9
  62.4 0.6 copy.10

commit v11 on v10

--- a/solution.py
+++ b/solution.py
@@ -160,10 +160,10 @@
     def sib_arrive(u):
         took(sib_recv.at[u // 8, u % 8], rows.at[pl.ds(0, PART)])
 
-    def squares(half):
-        @pl.loop(0, 4)
+    def squares(lo, hi):
+        @pl.loop(lo, hi)
         def _(i):
-            at = pl.ds(pl.multiple_of(half * 512 + i * CENTS, CENTS), CENTS)
+            at = pl.ds(pl.multiple_of(i * CENTS, CENTS), CENTS)
             c = cents[at, :].astype(jnp.float32)
             total = jnp.sum(c * c, axis=1, keepdims=True) * (0.5 * ALPHA)
             half_sq[at, :] = jnp.broadcast_to(total, (CENTS, 128))
@@ -299,6 +299,7 @@
     sib_copy(1, 0).start()
     own[0].wait()
     own[1].wait()
+    squares(0, 1)
     cent_arrive(0)
     cent_start(3)
     cent_start(4)
@@ -310,7 +311,7 @@
     row_arrive(0, 1)
     row_start(0, 5)
     cent_arrive(2)
-    squares(0)
+    squares(1, 4)
     row_arrive(0, 2)
 
     first = (0, 8, 1, 2, 3, 4, 5, 6)
@@ -334,6 +335,7 @@
             row_start(1, 2)
             cent_arrive(5)
         if i == 7:
+            squares(4, 7)
             row_arrive(0, 6)
         sib_arrive(first[i])
 
@@ -344,7 +346,7 @@
         score(first_unit(i), (0, 1), True)
 
     cent_arrive(6)
-    squares(1)
+    squares(7, 8)
     score(0, (2, 3), False)
 
     @pl.loop(1, 8)

time: 63.8 us -> 63.3 us (level)
  no operation moved by 1% of the time
where the time goes in v11:
time: 63.3 us; the launch traced here: 62.6 us
  Pallas kernels  60.1 us (95%)
  local copies, waits for them, and re-layouts  1.87 us (3%)
  between operations  0.64 us (1%)
    pallas_call x1, Pallas kernels, local(): pl.pallas_call(kernel, out_shape=(vmem((CENTS, WIDTH), f32), vmem((CENTS,...  60.1 us
    unnamed x3, local copies, waits for them, and re-layouts  1.87 us

profile of v11, /device:TPU:1, one launch (start us, length us, event | category | flops | bytes accessed | tf_op | source)
XLA Modules:
  0.0 62.6 jit_solution(7814869079953579802)
XLA Ops:
  0.6 60.1 %shard_map.49 = (f32[128,1024]{1,0:T(8,128)S(1)}, f32[128]{0:T(128)S(1)}, f32[256]{0:T(256)S(1)}) custom-call(bf16[256,1024]{1,0:T(8,128)(2,1)} %emb.1, f32[128,1024]{1,0:T(8,128)} %book.1), custom_call_target="tpu_custom_call" | custom-call | flops 17179869184 | bytes 2097152 | tf_op jit(solution)/shard_map/pallas_call | solution.py:481
  60.8 0.8 %copy.8 = f32[128,1024]{1,0:T(8,128)} copy(f32[128,1024]{1,0:T(8,128)S(1)} %get-tuple-element.3) | data formatting | bytes 1048576
  61.6 0.5 copy.9
  62.1 0.6 copy.10
